TPU v7x, 32 devices: a whole 2x2x4 slice. The times are simulated.
32 devices in a mesh: view: 8 (over z, core), tile: 4 (over y, x).
Axes of the slice: x: 2, y: 2, z: 4, core: 2. Of those that a mesh axis runs over, the one named last changes fastest.
Arguments:
- params: float32 [59, 32768], P(None, ('view', 'tile')), may hold values from -25 to 25, as said below
- first: float32 [59, 32768], P(None, ('view', 'tile')), may hold values from -0.3 to 0.3
- second: float32 [59, 32768], P(None, ('view', 'tile')), may hold values from 0.0001 to 0.01
- visible: int32 [8, 2048], P(None, ('view', 'tile')), may hold values from 0 to 1023, as said below
- cameras: float32 [8, 11], replicated, as said below
- tile_lists: int32 [8, 8, 1024], P('view', 'tile'), may hold values from 0 to 2047
- tile_blocks: int32 [8, 8], P('view', 'tile'), may hold values from 1 to 8, as said below
- targets: float32 [8, 3, 2048], P('view', None, 'tile'), may hold values from 0 to 1
Outputs:
- new_params: float32 [59, 32768], P(None, ('view', 'tile'))
- new_first: float32 [59, 32768], P(None, ('view', 'tile'))
- new_second: float32 [59, 32768], P(None, ('view', 'tile'))
- rendered: float32 [8, 3, 2048], P('view', None, 'tile')
Inputs may be any that keep to these rules, and one draw needn't show every extreme that they name: `visible`: for each view and each owner (a run of 64 entries), distinct local columns of that owner. `tile_blocks`: number of live blocks of 128 entries at the head of each tile's list; the first tile of every view has all 8. `params`: rows 0 to 2 in -25 to 25; rows 3 to 5 in -6 to 2.5; row 6 in 1 to 2; rows 7 to 9 in -1 to 1; row 10 in -7.5 to -5.5; rows 11 to 58 in -1.2 to 1.2. `cameras`: column 0 in 0.5 to 1, columns 1 to 3 in -1 to 1, columns 4 and 5 in -0.3 to 0.3, column 6 in 6 to 9; focal lengths 0.7 to 1.1 times the larger side of the window of 128 by 16 pixels; the principal point within 8 pixels of the window's middle.
All inputs are finite; a program needn't handle non-finite values.
Results may differ from a plain program's by a relative error of at most 0.0003.
Values sent between devices are 32-bit elements; how exact they have to be, the bound alone decides.
A program may use at most 128 MiB of HBM per device.

v0:
```python
import jax
import jax.numpy as jnp
from jax import lax
from jax.sharding import PartitionSpec as P

SIDE = 16
PIX = 256
BLOCK = 128
WIN_COLS = 8


harm_zero = 0.28209479177387814
harm_one = 0.4886025119029199
harm_two = (
    1.0925484305920792,
    -1.0925484305920792,
    0.31539156525252005,
    -1.0925484305920792,
    0.5462742152960396,
)
harm_three = (
    -0.5900435899266435,
    2.890611442640554,
    -0.4570457994644658,
    0.3731763325901154,
    -0.4570457994644658,
    1.445305721320277,
    -0.5900435899266435,
)
learn_rate = 0.05
beta_first = 0.9
beta_second = 0.999
adam_eps = 1e-08
blur_add = 0.3


def rotation(real_part, axis_one, axis_two, axis_three):
    inverse = lax.rsqrt(
        real_part * real_part + axis_one * axis_one + axis_two * axis_two + axis_three * axis_three
    )
    real_unit = real_part * inverse
    unit_one = axis_one * inverse
    unit_two = axis_two * inverse
    unit_three = axis_three * inverse
    return (
        (
            1.0 - 2.0 * (unit_two * unit_two + unit_three * unit_three),
            2.0 * (unit_one * unit_two - real_unit * unit_three),
            2.0 * (unit_one * unit_three + real_unit * unit_two),
        ),
        (
            2.0 * (unit_one * unit_two + real_unit * unit_three),
            1.0 - 2.0 * (unit_one * unit_one + unit_three * unit_three),
            2.0 * (unit_two * unit_three - real_unit * unit_one),
        ),
        (
            2.0 * (unit_one * unit_three - real_unit * unit_two),
            2.0 * (unit_two * unit_three + real_unit * unit_one),
            1.0 - 2.0 * (unit_one * unit_one + unit_two * unit_two),
        ),
    )


def harmonics(first_dir, second_dir, third_dir):
    sq_first = first_dir * first_dir
    sq_second = second_dir * second_dir
    sq_third = third_dir * third_dir
    return [
        harm_zero,
        -harm_one * second_dir,
        harm_one * third_dir,
        -harm_one * first_dir,
        harm_two[0] * first_dir * second_dir,
        harm_two[1] * second_dir * third_dir,
        harm_two[2] * (2.0 * sq_third - sq_first - sq_second),
        harm_two[3] * first_dir * third_dir,
        harm_two[4] * (sq_first - sq_second),
        harm_three[0] * second_dir * (3.0 * sq_first - sq_second),
        harm_three[1] * first_dir * second_dir * third_dir,
        harm_three[2] * second_dir * (4.0 * sq_third - sq_first - sq_second),
        harm_three[3] * third_dir * (2.0 * sq_third - 3.0 * sq_first - 3.0 * sq_second),
        harm_three[4] * first_dir * (4.0 * sq_third - sq_first - sq_second),
        harm_three[5] * third_dir * (sq_first - sq_second),
        harm_three[6] * first_dir * (sq_first - 3.0 * sq_second),
    ]


def project(raw, camera):
    camera_turn = rotation(camera[0], camera[1], camera[2], camera[3])
    shift_vec = (camera[4], camera[5], camera[6])
    focal_x = camera[7]
    focal_y = camera[8]
    position = (raw[0], raw[1], raw[2])
    viewed = [
        camera_turn[across][0] * position[0]
        + camera_turn[across][1] * position[1]
        + camera_turn[across][2] * position[2]
        + shift_vec[across]
        for across in range(3)
    ]
    inverse = 1.0 / viewed[2]
    mean_x = focal_x * viewed[0] * inverse + camera[9]
    mean_y = focal_y * viewed[1] * inverse + camera[10]
    gauss_turn = rotation(raw[6], raw[7], raw[8], raw[9])
    stretch = [jnp.exp(raw[3 + column]) for column in range(3)]
    jac_xx = focal_x * inverse
    jac_xz = -focal_x * viewed[0] * inverse * inverse
    jac_yy = focal_y * inverse
    jac_yz = -focal_y * viewed[1] * inverse * inverse
    leading_x = [
        jac_xx * camera_turn[0][column] + jac_xz * camera_turn[2][column] for column in range(3)
    ]
    leading_y = [
        jac_yy * camera_turn[1][column] + jac_yz * camera_turn[2][column] for column in range(3)
    ]
    axes_x = [
        (
            leading_x[0] * gauss_turn[0][column]
            + leading_x[1] * gauss_turn[1][column]
            + leading_x[2] * gauss_turn[2][column]
        )
        * stretch[column]
        for column in range(3)
    ]
    axes_y = [
        (
            leading_y[0] * gauss_turn[0][column]
            + leading_y[1] * gauss_turn[1][column]
            + leading_y[2] * gauss_turn[2][column]
        )
        * stretch[column]
        for column in range(3)
    ]
    cov_xx = axes_x[0] * axes_x[0] + axes_x[1] * axes_x[1] + axes_x[2] * axes_x[2] + blur_add
    cov_xy = axes_x[0] * axes_y[0] + axes_x[1] * axes_y[1] + axes_x[2] * axes_y[2]
    cov_yy = axes_y[0] * axes_y[0] + axes_y[1] * axes_y[1] + axes_y[2] * axes_y[2] + blur_add
    determ = cov_xx * cov_yy - cov_xy * cov_xy
    opacity = jax.nn.sigmoid(raw[10])
    camera_eye = [
        -(
            camera_turn[0][column] * shift_vec[0]
            + camera_turn[1][column] * shift_vec[1]
            + camera_turn[2][column] * shift_vec[2]
        )
        for column in range(3)
    ]
    offset = [position[column] - camera_eye[column] for column in range(3)]
    length = lax.rsqrt(offset[0] * offset[0] + offset[1] * offset[1] + offset[2] * offset[2])
    harmonic_terms = harmonics(offset[0] * length, offset[1] * length, offset[2] * length)
    colours = []
    for channel in range(3):
        total = 0.5 + jnp.zeros_like(opacity)
        for harmonic in range(16):
            total = total + raw[11 + 16 * channel + harmonic] * harmonic_terms[harmonic]
        colours.append(total)
    return jnp.stack(
        [mean_x, mean_y, cov_yy / determ, -cov_xy / determ, cov_xx / determ, opacity] + colours
    )


def composite(rows, anchor_x, anchor_y, count):
    pixel = jnp.arange(PIX, dtype=jnp.int32)
    pixel_x = (anchor_x + (pixel % SIDE).astype(jnp.float32) + 0.5)[:, None]
    pixel_y = (anchor_y + (pixel // SIDE).astype(jnp.float32) + 0.5)[:, None]
    ahead = (
        lax.broadcasted_iota(jnp.int32, (BLOCK, BLOCK), 0)
        < lax.broadcasted_iota(jnp.int32, (BLOCK, BLOCK), 1)
    ).astype(jnp.float32)
    current = (jnp.zeros((PIX,), jnp.float32), jnp.zeros((3, PIX), jnp.float32))
    for block in range(rows.shape[1] // BLOCK):
        piece = rows[:, block * BLOCK : (block + 1) * BLOCK]
        live = (block < count).astype(jnp.float32)

        def advance(holder, piece=piece, live=live):
            carried, image = holder
            delta_x = pixel_x - piece[0][None, :]
            delta_y = pixel_y - piece[1][None, :]
            power = (
                piece[2][None, :] * delta_x * delta_x
                + 2.0 * piece[3][None, :] * delta_x * delta_y
                + piece[4][None, :] * delta_y * delta_y
            )
            alpha = piece[5][None, :] * jnp.exp(-0.5 * power) * live
            decay = jnp.log1p(-alpha)
            before = (
                jnp.dot(
                    decay,
                    ahead,
                    precision=lax.Precision.HIGHEST,
                    preferred_element_type=jnp.float32,
                )
                + carried[:, None]
            )
            weight = alpha * jnp.exp(before)
            image = image + lax.dot_general(
                piece[6:9],
                weight,
                (((1,), (1,)), ((), ())),
                precision=lax.Precision.HIGHEST,
                preferred_element_type=jnp.float32,
            )
            return (carried + jnp.sum(decay, axis=1), image)

        current = advance(current)
    return current[1]


def shards(params, first, second, visible, cameras, tile_lists, tile_blocks, targets):
    views = lax.axis_size("view")
    own_rows = visible.shape[1]
    width_params = params.shape[0]
    flat_ids = visible.reshape(-1)
    picked = jnp.take(params, flat_ids, axis=1).reshape(width_params, views, own_rows)
    outgoing, pullback = jax.vjp(
        lambda source: jax.vmap(project, in_axes=(1, 0), out_axes=1)(source, cameras), picked
    )
    projected = lax.all_to_all(outgoing, "view", split_axis=1, concat_axis=1, tiled=True).reshape(
        outgoing.shape[0], views * own_rows
    )
    everyone = lax.all_gather(projected, "tile", axis=1, tiled=True)
    per_device = tile_lists.shape[1]
    lists = tile_lists[0]
    counts = tile_blocks[0]
    wanted = jnp.transpose(targets[0].reshape(3, per_device, PIX), (1, 0, 2))
    first_tile = lax.axis_index("tile") * per_device

    def one_tile(inputs):
        offset_tile, listed, count, goal = inputs
        global_tile = first_tile + offset_tile
        anchor_x = (global_tile % WIN_COLS * SIDE).astype(jnp.float32)
        anchor_y = (global_tile // WIN_COLS * SIDE).astype(jnp.float32)
        rows = jnp.take(everyone, listed, axis=1)
        image, pull = jax.vjp(lambda source: composite(source, anchor_x, anchor_y, count), rows)
        (rows_grad,) = pull(2.0 * (image - goal))
        return (image, rows_grad)

    images, row_grads = lax.map(
        one_tile, (jnp.arange(per_device, dtype=jnp.int32), lists, counts, wanted)
    )
    spread = jnp.transpose(row_grads, (1, 0, 2)).reshape(everyone.shape[0], -1)
    gathered_grad = jnp.zeros(everyone.shape, jnp.float32).at[:, lists.reshape(-1)].add(spread)
    mine = lax.psum_scatter(gathered_grad, "tile", scatter_dimension=1, tiled=True)
    arrived = lax.all_to_all(
        mine.reshape(mine.shape[0], views, own_rows),
        "view",
        split_axis=1,
        concat_axis=1,
        tiled=True,
    )
    (returned,) = pullback(arrived)
    grad = (
        jnp.zeros(params.shape, jnp.float32).at[:, flat_ids].add(returned.reshape(width_params, -1))
    )
    hits = jnp.zeros((params.shape[1],), jnp.float32).at[flat_ids].add(1.0)
    seen = (hits > 0.5)[None, :]
    moved_first = beta_first * first + (1.0 - beta_first) * grad
    moved_second = beta_second * second + (1.0 - beta_second) * grad * grad
    moved_params = params - learn_rate * moved_first / (jnp.sqrt(moved_second) + adam_eps)
    new_first = jnp.where(seen, moved_first, first)
    new_second = jnp.where(seen, moved_second, second)
    new_params = jnp.where(seen, moved_params, params)
    rendered = jnp.transpose(images, (1, 0, 2)).reshape(1, 3, per_device * PIX)
    return (new_params, new_first, new_second, rendered)


def solution(mesh):
    in_specs = (
        P(None, ("view", "tile")),
        P(None, ("view", "tile")),
        P(None, ("view", "tile")),
        P(None, ("view", "tile")),
        P(),
        P("view", "tile", None),
        P("view", "tile"),
        P("view", None, "tile"),
    )
    out_specs = (
        P(None, ("view", "tile")),
        P(None, ("view", "tile")),
        P(None, ("view", "tile")),
        P("view", None, "tile"),
    )
    return jax.shard_map(shards, mesh=mesh, in_specs=in_specs, out_specs=out_specs, check_vma=False)
```

profile of v0, /device:TPU:0, one launch (start us, length us, event | category | flops | bytes accessed | tf_op | source)
XLA Modules:
  0.0 167.1 jit_solution(5899480834610030366)
XLA Ops:
  7.2 0.8 reshape.23184
  8.1 1.2 copy.118
  9.3 1.0 gather_fusion.1
  10.9 0.6 copy-done
  16.2 0.5 negate_reduce_fusion.2
  17.2 0.7 reshape.23612
  17.9 6.5 %all-to-all-start = ((f32[8,1,576]{2,1,0:T(1,128)}), f32[8,1,576]{2,1,0:T(1,128)S(1)}, u32[]{:S(2)}, u32[]{:S(2)}) async-start(f32[8,1,576]{2,1,0:T(1,128)} %reshape.23612), calls=%async_computation | async-start | bytes 40960 | tf_op jit(solution)/shard_map/all_to_all | solution.py:217
  24.5 0.6 copy-done.5
  25.2 4.9 %all-to-all-done = f32[8,1,576]{2,1,0:T(1,128)S(1)} async-done(((f32[8,1,576]{2,1,0:T(1,128)}), f32[8,1,576]{2,1,0:T(1,128)S(1)}, u32[]{:S(2)}, u32[]{:S(2)}) %all-to-all-start) | async-done | bytes 18464 | tf_op jit(solution)/shard_map/all_to_all | solution.py:217
  30.0 0.5 broadcast.11473
  30.5 0.7 reduce.375
  31.4 8.5 %all_gather.3 = f32[9,2048]{1,0:T(8,128)S(1)} all-gather(f32[9,512]{1,0:T(8,128)S(1)} %reshape.23186), channel_id=1, replica_groups=mesh['view'=8,'tile'=4] {'tile'}, dimensions={1}, use_global_device_ids=true | all-gather | bytes 92160 | tf_op jit(solution)/shard_map/all_gather | solution.py:220
  40.3 0.6 copy-done.6
  40.9 60.0 %while.15 = (s32[]{:T(128)}, f32[2,3,256]{2,1,0:T(4,128)S(1)}, f32[2,9,1024]{2,1,0:T(8,128)S(1)}, s32[2,1024]{1,0:T(2,128)S(1)}, f32[9,2048]{0,1:T(8,128)S(1)}, ...) while((s32[]{:T(128)}, f32[2,3,256]{2,1,0:T(4,128)S(1)}, ...), condition=%wide.region_64.65_spmd, body=%wide.region_1.64_spmd.sunk | while | flops 865354496 | bytes 8221440 | solution.py:237
  40.9 0.6 dynamic_slice.39
  42.2 2.8 %gather_fusion = f32[1024,9]{1,0:T(8,128)S(1)} fusion(f32[9,2048]{0,1:T(8,128)S(1)} %get-tuple-element.1008, s32[1024]{0:T(1024)S(1)} %broadcast_clamp_fusion.2), kind=kCustom, calls=%fused_computation.clone.1 | custom fusion | bytes 77824 | tf_op jit(solution)/shard_map/while/body/eval_jaxpr/jit(_take)/gather | solution.py:232
  45.3 0.7 slice_reduce_fusion.104
  46.0 0.6 dynamic_slice.38
  47.5 0.7 slice_reduce_fusion.103
  60.7 0.4 fusion.631
  61.1 0.5 fusion.632
  62.0 0.4 fusion.633
  62.4 0.5 fusion.634
  63.3 0.4 fusion.635
  63.7 0.5 fusion.636
  64.6 0.4 fusion.637
  65.0 0.5 fusion.638
  65.9 0.4 fusion.639
  66.3 0.5 fusion.640
  67.6 0.5 fusion.642
  68.9 0.5 fusion.644
  70.2 0.5 fusion.645
  70.8 0.6 dynamic_slice.39
  72.1 2.8 %gather_fusion = f32[1024,9]{1,0:T(8,128)S(1)} fusion(f32[9,2048]{0,1:T(8,128)S(1)} %get-tuple-element.1008, s32[1024]{0:T(1024)S(1)} %broadcast_clamp_fusion.2), kind=kCustom, calls=%fused_computation.clone.1 | custom fusion | bytes 77824 | tf_op jit(solution)/shard_map/while/body/eval_jaxpr/jit(_take)/gather | solution.py:232
  75.2 0.7 slice_reduce_fusion.104
  75.9 0.6 dynamic_slice.38
  77.4 0.7 slice_reduce_fusion.103
  90.6 0.4 fusion.631
  91.0 0.5 fusion.632
  91.9 0.4 fusion.633
  92.3 0.5 fusion.634
  93.6 0.5 fusion.636
  94.5 0.4 fusion.637
  94.9 0.5 fusion.638
  95.8 0.4 fusion.639
  96.2 0.5 fusion.640
  97.5 0.5 fusion.642
  98.8 0.5 fusion.644
  100.1 0.5 fusion.645
  101.4 12.5 %scatter_custom_fusion.1 = f32[9,2048]{0,1:T(8,128)} fusion(s32[2048]{0:T(1024)S(1)} %bitcast.364, f32[2048,9]{1,0:T(8,128)S(1)} %copy.105, f32[]{:T(128)} %constant.260.clone.1), kind=kCustom, calls=%fused_computation.567 | custom fusion | flops 18432 | bytes 73732 | tf_op jit(solution)/shard_map/scatter-add | solution.py:241
  114.0 4.1 %scatter_custom_fusion = f32[1024]{0:T(1024)S(1)} fusion(s32[512]{0:T(512)S(1)} %bitcast.362, f32[512]{0:T(512)S(1)} %broadcast.10376, f32[]{:T(128)} %constant.260.clone.1), kind=kCustom, calls=%fused_computation.899 | custom fusion | flops 512 | bytes 4100 | tf_op jit(solution)/shard_map/scatter-add | solution.py:254
  118.1 21.1 %reduce-scatter.2.cloned.1.call-done = f32[9,512]{0,1:T(8,128)} async-done(((f32[9,2048]{0,1:T(8,128)}), f32[9,512]{0,1:T(8,128)}) %reduce-scatter.2.cloned.1.call-update) | async-done | bytes 18448 | tf_op jit(solution)/shard_map/reduce_scatter | solution.py:242
  139.1 1.1 copy.106
  140.2 0.7 reshape.23614
  140.9 4.6 %all-to-all-start.1 = ((f32[8,1,576]{2,1,0:T(1,128)}), f32[8,1,576]{2,1,0:T(1,128)S(1)}, u32[]{:S(2)}, u32[]{:S(2)}) async-start(f32[8,1,576]{2,1,0:T(1,128)} %reshape.23614), calls=%async_computation.2 | async-start | bytes 40960 | tf_op jit(solution)/shard_map/all_to_all | solution.py:243
  145.8 0.7 copy-done.2
  146.7 0.6 reshape.23190
  147.3 3.9 %all-to-all-done.1 = f32[8,1,576]{2,1,0:T(1,128)S(1)} async-done(((f32[8,1,576]{2,1,0:T(1,128)}), f32[8,1,576]{2,1,0:T(1,128)S(1)}, u32[]{:S(2)}, u32[]{:S(2)}) %all-to-all-start.1) | async-done | bytes 18464 | tf_op jit(solution)/shard_map/all_to_all | solution.py:243
  151.2 0.7 reduce.376
  152.9 2.4 %scatter_custom_fusion.2 = f32[59,1024]{0,1:T(8,128)S(1)} fusion(s32[512]{0:T(512)S(1)} %bitcast.363, f32[512,59]{1,0:T(8,128)S(1)} %bitcast.315, f32[]{:T(128)} %constant.260.clone.1), kind=kCustom, calls=%fused_computation.571 | custom fusion | flops 30208 | bytes 241668 | tf_op jit(solution)/shard_map/scatter-add | solution.py:252
  155.3 1.2 fusion.349
  156.5 1.9 %copy.123 = f32[59,1024]{1,0:T(8,128)} copy(f32[59,1024]{0,1:T(8,128)} %get-tuple-element.516) | data formatting | bytes 483328
  158.4 0.9 copy.124
  159.3 0.9 copy.125
  (284 shorter events, 32.9 us)
Async XLA Ops:
  7.2 0.8 copy-start.4
  10.8 0.7 copy-start
  17.9 6.5 %copy-start.3 = (s32[1,2,1024]{2,1,0:T(2,128)S(1)}, s32[1,2,1024]{2,1,0:T(2,128)}, u32[]{:S(2)}) copy-start(s32[1,2,1024]{2,1,0:T(2,128)} %param.15) | copy-start | bytes 24580
  17.9 12.1 %all-to-all-start = ((f32[8,1,576]{2,1,0:T(1,128)}), f32[8,1,576]{2,1,0:T(1,128)S(1)}, u32[]{:S(2)}, u32[]{:S(2)}) async-start(f32[8,1,576]{2,1,0:T(1,128)} %reshape.23612), calls=%async_computation | async-start | bytes 40960 | tf_op jit(solution)/shard_map/all_to_all | solution.py:217
  24.3 114.8 %reduce-scatter.2.cloned.1.call-start = ((), (), s32[]{:S(2)}) async-start(), calls=%async_computation.3 | async-start | bytes 1310720 | tf_op jit(solution)/shard_map/reduce_scatter | solution.py:242
  24.4 0.7 copy-start.5
  40.2 0.7 copy-start.6
  113.9 31.6 %copy-start.1 = (f32[59,1024]{1,0:T(8,128)S(1)}, f32[59,1024]{1,0:T(8,128)}, u32[]{:S(2)}) copy-start(f32[59,1024]{1,0:T(8,128)} %param.12) | copy-start | bytes 724996
  140.9 10.3 %all-to-all-start.1 = ((f32[8,1,576]{2,1,0:T(1,128)}), f32[8,1,576]{2,1,0:T(1,128)S(1)}, u32[]{:S(2)}, u32[]{:S(2)}) async-start(f32[8,1,576]{2,1,0:T(1,128)} %reshape.23614), calls=%async_computation.2 | async-start | bytes 40960 | tf_op jit(solution)/shard_map/all_to_all | solution.py:243
  145.6 1.0 copy-start.2
Sparse Core Ops, SparseCore 0:
  114.1 25.0 reduce-scatter.1
where the time goes:
time: 168 us; the launch traced here: 167 us
  matrix products  31.4 us (19%)
  other arithmetic  31.3 us (19%)
  waiting for transfers between devices  29.8 us (18%)
  local copies, waits for them, and re-layouts  27.5 us (16%)
  between operations  14.4 us (9%)
  loops' own time  13.1 us (8%)
  starting transfers between devices  11.1 us (7%)
  blocking collectives  8.46 us (5%)
    reduce_scatter x1, waiting for transfers between devices, shards(): lax.psum_scatter(gathered_grad, 'tile', scatter_dimension=1, tiled=True)  21.1 us
    dot_general x48, matrix products, advance(): lax.dot_general(piece[6:9], weight, (((1,), (1,)), ((), ())), precision=l...  18.1 us
    dot_general x32, matrix products, advance(): jnp.dot(decay, ahead, precision=lax.Precision.HIGHEST, preferred_element_...  13.3 us
    another operation x1, loops' own time, shards(): lax.map(one_tile, (jnp.arange(per_device, dtype=jnp.int32), lists, counts...  13.1 us
    scatter-add x1, other arithmetic, shards(): jnp.zeros(everyone.shape, jnp.float32).at[:, lists.reshape(-1)].add(spread)  12.5 us
    unnamed x28, local copies, waits for them, and re-layouts  9.57 us
    all_gather x1, blocking collectives, shards(): everyone = lax.all_gather(projected, 'tile', axis=1, tiled=True)  8.46 us
    all_to_all x1, starting transfers between devices, shards(): lax.all_to_all(outgoing, 'view', split_axis=1, concat_axis=1, tiled=True)  6.46 us
  transfers between devices with their start and end apart: 3, of which 3 were waited for; matrix products, arithmetic and copies ran while one was open for 3% of the time, Pallas kernels for 0%

commit v1 on v0

v1 whole, which is shorter than its diff:
```python
import functools

import jax
import jax.numpy as jnp
from jax import lax
from jax.experimental import pallas as pl
from jax.experimental.pallas import tpu as pltpu
from jax.sharding import PartitionSpec as P

SIDE = 16
PIX = 256
BLOCK = 128
WIN_COLS = 8
SUBS = 8
MESH = pl.DeviceIdType.MESH
VMEM = pl.BlockSpec(memory_space=pltpu.VMEM)
SMEM = pl.BlockSpec(memory_space=pltpu.SMEM)
LIMIT = 48 * 1024 * 1024


harm_zero = 0.28209479177387814
harm_one = 0.4886025119029199
harm_two = (
    1.0925484305920792,
    -1.0925484305920792,
    0.31539156525252005,
    -1.0925484305920792,
    0.5462742152960396,
)
harm_three = (
    -0.5900435899266435,
    2.890611442640554,
    -0.4570457994644658,
    0.3731763325901154,
    -0.4570457994644658,
    1.445305721320277,
    -0.5900435899266435,
)
learn_rate = 0.05
beta_first = 0.9
beta_second = 0.999
adam_eps = 1e-08
blur_add = 0.3


def rotation(real_part, axis_one, axis_two, axis_three):
    inverse = lax.rsqrt(
        real_part * real_part + axis_one * axis_one + axis_two * axis_two + axis_three * axis_three
    )
    real_unit = real_part * inverse
    unit_one = axis_one * inverse
    unit_two = axis_two * inverse
    unit_three = axis_three * inverse
    return (
        (
            1.0 - 2.0 * (unit_two * unit_two + unit_three * unit_three),
            2.0 * (unit_one * unit_two - real_unit * unit_three),
            2.0 * (unit_one * unit_three + real_unit * unit_two),
        ),
        (
            2.0 * (unit_one * unit_two + real_unit * unit_three),
            1.0 - 2.0 * (unit_one * unit_one + unit_three * unit_three),
            2.0 * (unit_two * unit_three - real_unit * unit_one),
        ),
        (
            2.0 * (unit_one * unit_three - real_unit * unit_two),
            2.0 * (unit_two * unit_three + real_unit * unit_one),
            1.0 - 2.0 * (unit_one * unit_one + unit_two * unit_two),
        ),
    )


def harmonics(first_dir, second_dir, third_dir):
    sq_first = first_dir * first_dir
    sq_second = second_dir * second_dir
    sq_third = third_dir * third_dir
    return [
        harm_zero,
        -harm_one * second_dir,
        harm_one * third_dir,
        -harm_one * first_dir,
        harm_two[0] * first_dir * second_dir,
        harm_two[1] * second_dir * third_dir,
        harm_two[2] * (2.0 * sq_third - sq_first - sq_second),
        harm_two[3] * first_dir * third_dir,
        harm_two[4] * (sq_first - sq_second),
        harm_three[0] * second_dir * (3.0 * sq_first - sq_second),
        harm_three[1] * first_dir * second_dir * third_dir,
        harm_three[2] * second_dir * (4.0 * sq_third - sq_first - sq_second),
        harm_three[3] * third_dir * (2.0 * sq_third - 3.0 * sq_first - 3.0 * sq_second),
        harm_three[4] * first_dir * (4.0 * sq_third - sq_first - sq_second),
        harm_three[5] * third_dir * (sq_first - sq_second),
        harm_three[6] * first_dir * (sq_first - 3.0 * sq_second),
    ]


def project(raw, camera):
    camera_turn = rotation(camera[0], camera[1], camera[2], camera[3])
    shift_vec = (camera[4], camera[5], camera[6])
    focal_x = camera[7]
    focal_y = camera[8]
    position = (raw[0], raw[1], raw[2])
    viewed = [
        camera_turn[across][0] * position[0]
        + camera_turn[across][1] * position[1]
        + camera_turn[across][2] * position[2]
        + shift_vec[across]
        for across in range(3)
    ]
    inverse = 1.0 / viewed[2]
    mean_x = focal_x * viewed[0] * inverse + camera[9]
    mean_y = focal_y * viewed[1] * inverse + camera[10]
    gauss_turn = rotation(raw[6], raw[7], raw[8], raw[9])
    stretch = [jnp.exp(raw[3 + column]) for column in range(3)]
    jac_xx = focal_x * inverse
    jac_xz = -focal_x * viewed[0] * inverse * inverse
    jac_yy = focal_y * inverse
    jac_yz = -focal_y * viewed[1] * inverse * inverse
    leading_x = [
        jac_xx * camera_turn[0][column] + jac_xz * camera_turn[2][column] for column in range(3)
    ]
    leading_y = [
        jac_yy * camera_turn[1][column] + jac_yz * camera_turn[2][column] for column in range(3)
    ]
    axes_x = [
        (
            leading_x[0] * gauss_turn[0][column]
            + leading_x[1] * gauss_turn[1][column]
            + leading_x[2] * gauss_turn[2][column]
        )
        * stretch[column]
        for column in range(3)
    ]
    axes_y = [
        (
            leading_y[0] * gauss_turn[0][column]
            + leading_y[1] * gauss_turn[1][column]
            + leading_y[2] * gauss_turn[2][column]
        )
        * stretch[column]
        for column in range(3)
    ]
    cov_xx = axes_x[0] * axes_x[0] + axes_x[1] * axes_x[1] + axes_x[2] * axes_x[2] + blur_add
    cov_xy = axes_x[0] * axes_y[0] + axes_x[1] * axes_y[1] + axes_x[2] * axes_y[2]
    cov_yy = axes_y[0] * axes_y[0] + axes_y[1] * axes_y[1] + axes_y[2] * axes_y[2] + blur_add
    determ = cov_xx * cov_yy - cov_xy * cov_xy
    opacity = 1.0 / (1.0 + jnp.exp(-raw[10]))
    camera_eye = [
        -(
            camera_turn[0][column] * shift_vec[0]
            + camera_turn[1][column] * shift_vec[1]
            + camera_turn[2][column] * shift_vec[2]
        )
        for column in range(3)
    ]
    offset = [position[column] - camera_eye[column] for column in range(3)]
    length = lax.rsqrt(offset[0] * offset[0] + offset[1] * offset[1] + offset[2] * offset[2])
    harmonic_terms = harmonics(offset[0] * length, offset[1] * length, offset[2] * length)
    colours = []
    for channel in range(3):
        total = 0.5 + jnp.zeros_like(opacity)
        for harmonic in range(16):
            total = total + raw[11 + 16 * channel + harmonic] * harmonic_terms[harmonic]
        colours.append(total)
    return [mean_x, mean_y, cov_yy / determ, -cov_xy / determ, cov_xx / determ, opacity] + colours


def three_pieces(value):
    high = value.astype(jnp.bfloat16)
    rest = value - high.astype(jnp.float32)
    middle = rest.astype(jnp.bfloat16)
    low = (rest - middle.astype(jnp.float32)).astype(jnp.bfloat16)
    return high, middle, low


def two_pieces(value):
    high = value.astype(jnp.bfloat16)
    return high, (value - high.astype(jnp.float32)).astype(jnp.bfloat16)


def matmul(left, right):
    return jnp.dot(left, right, preferred_element_type=jnp.float32)


def matmul_nt(left, right):
    return lax.dot_general(
        left, right, (((1,), (1,)), ((), ())), preferred_element_type=jnp.float32
    )


def column_hot(visible_ref, columns):
    views = visible_ref.shape[0]
    ids = jnp.concatenate([visible_ref[view : view + 1, :] for view in range(views)], axis=1)
    place = lax.broadcasted_iota(jnp.int32, (columns, ids.shape[1]), 0)
    return jnp.where(place == ids, 1.0, 0.0).astype(jnp.bfloat16)


def camera_rows(cameras_ref, own_rows):
    views = cameras_ref.shape[0]
    lane = lax.broadcasted_iota(jnp.int32, (1, views * own_rows), 1)
    rows = []
    for entry in range(11):
        row = jnp.full(lane.shape, cameras_ref[0, entry], jnp.float32)
        for view in range(1, views):
            row = jnp.where(lane >= view * own_rows, cameras_ref[view, entry], row)
        rows.append(row)
    return rows


def send_kernel(
    views, tiles, params_ref, visible_ref, cameras_ref, all_ref, picked_ref, outgoing,
    view_send, view_recv, tile_send, tile_recv
):
    my_view, my_tile = lax.axis_index("view"), lax.axis_index("tile")
    barrier = pltpu.get_barrier_semaphore()
    for step in range(1, views):
        pl.semaphore_signal(
            barrier, inc=1, device_id=(lax.rem(my_view + step, views), my_tile), device_id_type=MESH
        )
    for step in range(1, tiles):
        pl.semaphore_signal(
            barrier, inc=1, device_id=(my_view, lax.rem(my_tile + step, tiles)), device_id_type=MESH
        )
    width, columns = params_ref.shape
    own_rows = visible_ref.shape[1]
    hot = column_hot(visible_ref, columns)
    padded = jnp.concatenate(
        [params_ref[...], jnp.zeros((64 - width, columns), jnp.float32)], axis=0
    )
    parts = matmul(jnp.concatenate(three_pieces(padded), axis=0), hot)
    picked_ref[...] = parts[0:64] + parts[64:128] + parts[128:192]
    cameras = camera_rows(cameras_ref, own_rows)
    raw = [picked_ref[row : row + 1, :] for row in range(width)]
    out = project(raw, cameras)
    zero = jnp.zeros_like(out[0])
    lower = jnp.concatenate(out[0:4] + [out[8], zero, zero, zero], axis=0)
    upper = jnp.concatenate(out[4:8] + [zero, zero, zero, zero], axis=0)
    for view in range(views):
        span = slice(view * own_rows, (view + 1) * own_rows)
        outgoing[view] = jnp.concatenate([lower[:, span], upper[:, span]], axis=1)
    pl.semaphore_wait(barrier, views + tiles - 2)
    for step in range(1, views):
        other = lax.rem(my_view + step, views)
        pltpu.make_async_remote_copy(
            src_ref=outgoing.at[other], dst_ref=all_ref.at[my_tile, my_view],
            send_sem=view_send.at[other], recv_sem=view_recv.at[my_view],
            device_id=(other, my_tile), device_id_type=MESH,
        ).start()
    all_ref[my_tile, my_view] = outgoing[my_view]
    for step in range(1, views):
        other = lax.rem(my_view + step, views)
        pltpu.make_async_remote_copy(
            src_ref=outgoing.at[other], dst_ref=all_ref.at[my_tile, other],
            send_sem=view_send.at[other], recv_sem=view_recv.at[other],
            device_id=(other, my_tile), device_id_type=MESH,
        ).wait_recv()
    for step in range(1, tiles):
        other = lax.rem(my_tile + step, tiles)
        pltpu.make_async_remote_copy(
            src_ref=all_ref.at[my_tile], dst_ref=all_ref.at[my_tile],
            send_sem=tile_send.at[other], recv_sem=tile_recv.at[my_tile],
            device_id=(my_view, other), device_id_type=MESH,
        ).start()
    for step in range(1, views):
        other = lax.rem(my_view + step, views)
        pltpu.make_async_remote_copy(
            src_ref=outgoing.at[other], dst_ref=all_ref.at[my_tile, my_view],
            send_sem=view_send.at[other], recv_sem=view_recv.at[my_view],
            device_id=(other, my_tile), device_id_type=MESH,
        ).wait_send()
    for step in range(1, tiles):
        other = lax.rem(my_tile + step, tiles)
        copy = pltpu.make_async_remote_copy(
            src_ref=all_ref.at[my_tile], dst_ref=all_ref.at[other],
            send_sem=tile_send.at[other], recv_sem=tile_recv.at[other],
            device_id=(my_view, other), device_id_type=MESH,
        )
        copy.wait_send()
        copy.wait_recv()


def return_kernel(
    views, tiles, given_ref, out_ref, landed, summed, view_send, view_recv, tile_send, tile_recv
):
    my_view, my_tile = lax.axis_index("view"), lax.axis_index("tile")
    barrier = pltpu.get_barrier_semaphore()
    for step in range(1, views):
        pl.semaphore_signal(
            barrier, inc=1, device_id=(lax.rem(my_view + step, views), my_tile), device_id_type=MESH
        )
    for step in range(1, tiles):
        pl.semaphore_signal(
            barrier, inc=1, device_id=(my_view, lax.rem(my_tile + step, tiles)), device_id_type=MESH
        )
    pl.semaphore_wait(barrier, views + tiles - 2)
    for step in range(1, tiles):
        other = lax.rem(my_tile + step, tiles)
        pltpu.make_async_remote_copy(
            src_ref=given_ref.at[other], dst_ref=landed.at[my_tile],
            send_sem=tile_send.at[other], recv_sem=tile_recv.at[my_tile],
            device_id=(my_view, other), device_id_type=MESH,
        ).start()
    total = given_ref[my_tile]
    for step in range(1, tiles):
        other = lax.rem(my_tile + step, tiles)
        pltpu.make_async_remote_copy(
            src_ref=given_ref.at[other], dst_ref=landed.at[other],
            send_sem=tile_send.at[other], recv_sem=tile_recv.at[other],
            device_id=(my_view, other), device_id_type=MESH,
        ).wait_recv()
        total = total + landed[other]
    summed[...] = total
    for step in range(1, views):
        other = lax.rem(my_view + step, views)
        pltpu.make_async_remote_copy(
            src_ref=summed.at[other], dst_ref=out_ref.at[my_view],
            send_sem=view_send.at[other], recv_sem=view_recv.at[my_view],
            device_id=(other, my_tile), device_id_type=MESH,
        ).start()
    out_ref[my_view] = summed[my_view]
    for step in range(1, tiles):
        other = lax.rem(my_tile + step, tiles)
        pltpu.make_async_remote_copy(
            src_ref=given_ref.at[other], dst_ref=landed.at[my_tile],
            send_sem=tile_send.at[other], recv_sem=tile_recv.at[my_tile],
            device_id=(my_view, other), device_id_type=MESH,
        ).wait_send()
    for step in range(1, views):
        other = lax.rem(my_view + step, views)
        copy = pltpu.make_async_remote_copy(
            src_ref=summed.at[other], dst_ref=out_ref.at[other],
            send_sem=view_send.at[other], recv_sem=view_recv.at[other],
            device_id=(other, my_tile), device_id_type=MESH,
        )
        copy.wait_send()
        copy.wait_recv()


def list_hot(lists_ref, tile, own_rows):
    ids = lists_ref[tile : tile + 1, :]
    place = lax.broadcasted_iota(jnp.int32, (2 * own_rows, ids.shape[1]), 0)
    low_ids = lax.rem(ids, own_rows)
    lower = jnp.where(place == low_ids, 1.0, 0.0).astype(jnp.bfloat16)
    upper = jnp.where(place == low_ids + own_rows, 1.0, 0.0).astype(jnp.bfloat16)
    return lax.div(ids, own_rows), lower, upper


def composite_kernel(
    owners, chunk, all_ref, lists_ref, counts_ref, targets_ref, given_ref, image_ref,
    rows, grads, weights, weight_parts, ratios, carried, held
):
    tiles = lists_ref.shape[0]
    entries = lists_ref.shape[1]
    own_rows = all_ref.shape[1] // 2
    chunk_rows = chunk * SUBS
    most = counts_ref[0, 0]
    for tile in range(1, tiles):
        most = jnp.maximum(most, counts_ref[0, tile])

    for tile in range(tiles):
        owner_ids, lower, upper = list_hot(lists_ref, tile, own_rows)
        lower3 = jnp.concatenate([lower] * 3, axis=0)
        upper3 = jnp.concatenate([upper] * 3, axis=0)

        def gather(index, held_rows):
            start = pl.multiple_of(index * chunk_rows, chunk_rows)
            source = jnp.concatenate(three_pieces(all_ref[pl.ds(start, chunk_rows), :]), axis=1)
            found_low = matmul(source, lower3)
            found_up = matmul(source, upper3)
            low, up = held_rows
            for owner in range(chunk):
                mine = (owner_ids == index * chunk + owner).astype(jnp.float32)
                span = slice(owner * SUBS, (owner + 1) * SUBS)
                low = low + found_low[span] * mine
                up = up + found_up[span] * mine
            return low, up

        empty = jnp.zeros((SUBS, entries), jnp.float32)
        low, up = lax.fori_loop(0, owners // chunk, gather, (empty, empty))
        rows[tile, 0:SUBS, :] = low
        rows[tile, SUBS : 2 * SUBS, :] = up

    first_tile = lax.axis_index("tile") * tiles
    half = SIDE // 2
    middles = []
    for tile in range(tiles):
        number = first_tile + tile
        middles.append(
            (
                (lax.rem(number, WIN_COLS) * SIDE + half).astype(jnp.float32),
                (lax.div(number, WIN_COLS) * SIDE + half).astype(jnp.float32),
            )
        )
    side_x = lax.broadcasted_iota(jnp.int32, (SIDE, BLOCK), 0).astype(jnp.float32) + (0.5 - half)
    spot = lax.broadcasted_iota(jnp.int32, (2 * BLOCK, 2 * BLOCK), 0) % BLOCK
    lane = lax.broadcasted_iota(jnp.int32, (2 * BLOCK, 2 * BLOCK), 1)
    ahead = jnp.where((spot < lane) | (lane >= BLOCK), 1.0, 0.0).astype(jnp.bfloat16)
    behind = jnp.where((spot > lane) | (lane >= BLOCK), 1.0, 0.0).astype(jnp.bfloat16)

    carried[...] = jnp.zeros_like(carried)
    held[...] = jnp.zeros_like(held)
    grads[...] = jnp.zeros_like(grads)

    def forward(block, _):
        start = pl.multiple_of(block * BLOCK, BLOCK)
        for tile in range(tiles):
            live = (block < counts_ref[0, tile]).astype(jnp.float32)
            low = rows[tile, 0:SUBS, pl.ds(start, BLOCK)]
            up = rows[tile, SUBS : 2 * SUBS, pl.ds(start, BLOCK)]
            mean_x = low[0:1] - middles[tile][0]
            mean_y = low[1:2] - middles[tile][1]
            form_a = -0.5 * low[2:3]
            form_b = -low[3:4]
            form_c = -0.5 * up[0:1]
            opacity = up[1:2] * live
            delta_x = side_x - mean_x
            square = form_a * delta_x * delta_x
            cross = form_b * delta_x
            pieces = []
            for line in range(SIDE):
                delta_y = (line + 0.5 - half) - mean_y
                pieces.append((cross + form_c * delta_y) * delta_y + square)
            alpha = opacity * jnp.exp(jnp.concatenate(pieces, axis=0))
            decay = jnp.log(1.0 - alpha)
            before = matmul(jnp.concatenate(two_pieces(decay), axis=1), ahead)
            past = carried[tile]
            weight = alpha * jnp.exp(before[:, 0:BLOCK] + past)
            carried[tile] = past + before[:, BLOCK:]
            ratios[tile, block] = alpha * jnp.exp(-decay)
            weights[tile, block] = weight
            parts = jnp.concatenate(two_pieces(weight), axis=1)
            weight_parts[tile, block] = parts
            colour = jnp.concatenate([up[2:4], low[4:5], jnp.zeros((5, BLOCK), jnp.float32)], axis=0)
            high = colour.astype(jnp.bfloat16).astype(jnp.float32)
            both = jnp.concatenate([high, colour - high], axis=0).astype(jnp.bfloat16)
            held[tile] += matmul_nt(parts, jnp.concatenate([both, both], axis=1))
        return 0

    lax.fori_loop(0, most, forward, 0)

    slopes, slopes_wide = [], []
    for tile in range(tiles):
        drawn = jnp.transpose(
            jnp.concatenate(
                [held[tile], jnp.zeros((PIX, BLOCK - 2 * SUBS), jnp.float32)], axis=1
            )
        )
        drawn = drawn[0:3] + drawn[SUBS : SUBS + 3]
        image_ref[:, tile * PIX : (tile + 1) * PIX] = drawn
        slope = 2.0 * (drawn - targets_ref[:, tile * PIX : (tile + 1) * PIX])
        high = slope.astype(jnp.bfloat16).astype(jnp.float32)
        stack = jnp.concatenate(
            [high, slope - high, high, jnp.zeros((BLOCK - 9, PIX), jnp.float32)], axis=0
        )
        slopes.append(stack[0 : 2 * SUBS].astype(jnp.bfloat16))
        slopes_wide.append(jnp.transpose(stack).astype(jnp.bfloat16)[:, 0 : 2 * SUBS])

    pixel = lax.broadcasted_iota(jnp.int32, (2 * SUBS, PIX), 1)
    kind = lax.broadcasted_iota(jnp.int32, (2 * SUBS, PIX), 0)
    at_x = (pixel % SIDE).astype(jnp.float32) + (0.5 - half)
    at_y = (pixel // SIDE).astype(jnp.float32) + (0.5 - half)
    power_x = jnp.where((kind == 1) | (kind == 4), at_x, jnp.where(kind == 3, at_x * at_x, 1.0))
    power_y = jnp.where((kind == 2) | (kind == 4), at_y, jnp.where(kind == 5, at_y * at_y, 1.0))
    basis = jnp.where(kind < 6, power_x * power_y, 0.0).astype(jnp.bfloat16)

    carried[...] = jnp.zeros_like(carried)

    def backward(index, _):
        block = most - 1 - index
        start = pl.multiple_of(block * BLOCK, BLOCK)
        for tile in range(tiles):
            low = rows[tile, 0:SUBS, pl.ds(start, BLOCK)]
            up = rows[tile, SUBS : 2 * SUBS, pl.ds(start, BLOCK)]
            colour = jnp.concatenate([up[2:4], low[4:5]], axis=0)
            high = colour.astype(jnp.bfloat16).astype(jnp.float32)
            both = jnp.concatenate(
                [high, high, colour - high, jnp.zeros((7, BLOCK), jnp.float32)], axis=0
            ).astype(jnp.bfloat16)
            pulled = matmul(slopes_wide[tile], both) * weights[tile, block]
            after = matmul(jnp.concatenate(two_pieces(pulled), axis=1), behind)
            past = carried[tile]
            inner = pulled - (after[:, 0:BLOCK] + past) * ratios[tile, block]
            carried[tile] = past + after[:, BLOCK:]
            inner_high, inner_low = two_pieces(inner)
            sums = matmul(basis, inner_high) + matmul(basis, inner_low)
            parts = weight_parts[tile, block]
            tint = matmul(slopes[tile], parts[:, 0:BLOCK])
            tint_low = matmul(slopes[tile], parts[:, BLOCK:])
            tint = tint[0:3] + tint[3:6] + tint_low[0:3]
            mean_x = low[0:1] - middles[tile][0]
            mean_y = low[1:2] - middles[tile][1]
            form_a, form_b, form_c = low[2:3], low[3:4], up[0:1]
            whole, by_x, by_y = sums[0:1], sums[1:2], sums[2:3]
            sum_x = by_x - mean_x * whole
            sum_y = by_y - mean_y * whole
            sum_xx = sums[3:4] - 2.0 * mean_x * by_x + mean_x * mean_x * whole
            sum_xy = sums[4:5] - mean_x * by_y - mean_y * by_x + mean_x * mean_y * whole
            sum_yy = sums[5:6] - 2.0 * mean_y * by_y + mean_y * mean_y * whole
            zeros = jnp.zeros((4, BLOCK), jnp.float32)
            grads[tile, 0:SUBS, pl.ds(start, BLOCK)] = jnp.concatenate(
                [
                    form_a * sum_x + form_b * sum_y,
                    form_b * sum_x + form_c * sum_y,
                    -0.5 * sum_xx,
                    -sum_xy,
                    tint[2:3],
                    zeros[0:3],
                ],
                axis=0,
            )
            grads[tile, SUBS : 2 * SUBS, pl.ds(start, BLOCK)] = jnp.concatenate(
                [-0.5 * sum_yy, whole / up[1:2], tint[0:2], zeros], axis=0
            )
        return 0

    lax.fori_loop(0, most, backward, 0)

    def scatter(index, _):
        begin = pl.multiple_of(index * chunk_rows, chunk_rows)
        total = jnp.zeros((chunk_rows, 2 * own_rows), jnp.float32)
        owner = lax.broadcasted_iota(jnp.int32, (chunk_rows, entries), 0) // SUBS + index * chunk
        for tile in range(tiles):
            owner_ids, lower, upper = list_hot(lists_ref, tile, own_rows)
            mine = owner == owner_ids
            for part, hot in ((0, lower), (1, upper)):
                values = grads[tile, part * SUBS : (part + 1) * SUBS, :]
                high = values.astype(jnp.bfloat16).astype(jnp.float32)
                for piece in (high, values - high):
                    spread = jnp.concatenate([piece] * chunk, axis=0)
                    total = total + matmul_nt(
                        jnp.where(mine, spread, 0.0).astype(jnp.bfloat16), hot
                    )
        given_ref[pl.ds(begin, chunk_rows), :] = total
        return 0

    lax.fori_loop(0, owners // chunk, scatter, 0)


def update_kernel(
    params_ref, first_ref, second_ref, visible_ref, cameras_ref, picked_ref, arrived_ref,
    new_params_ref, new_first_ref, new_second_ref, slopes
):
    width, columns = params_ref.shape
    views, own_rows = visible_ref.shape
    lower = jnp.concatenate([arrived_ref[view][:, 0:own_rows] for view in range(views)], axis=1)
    upper = jnp.concatenate([arrived_ref[view][:, own_rows:] for view in range(views)], axis=1)
    cotangent = [lower[row : row + 1] for row in range(4)]
    cotangent += [upper[row : row + 1] for row in range(4)]
    cotangent += [lower[4:5]]
    cameras = camera_rows(cameras_ref, own_rows)
    raw = [picked_ref[row : row + 1, :] for row in range(width)]
    _, pullback = jax.vjp(lambda source: project(source, cameras), raw)
    (returned,) = pullback(cotangent)
    slopes[...] = jnp.ones_like(slopes)
    for row in range(width):
        slopes[row : row + 1, :] = returned[row]
    hot = column_hot(visible_ref, columns)
    parts = matmul_nt(jnp.concatenate(three_pieces(slopes[...]), axis=0), hot)
    grad = parts[0:64] + parts[64:128] + parts[128:192]
    seen = grad[width : width + 1] > 0.5
    grad = grad[0:width]
    first, second, params = first_ref[...], second_ref[...], params_ref[...]
    moved_first = beta_first * first + (1.0 - beta_first) * grad
    moved_second = beta_second * second + (1.0 - beta_second) * grad * grad
    moved_params = params - learn_rate * moved_first / (jnp.sqrt(moved_second) + adam_eps)
    new_first_ref[...] = jnp.where(seen, moved_first, first)
    new_second_ref[...] = jnp.where(seen, moved_second, second)
    new_params_ref[...] = jnp.where(seen, moved_params, params)


def shards(views, tiles, params, first, second, visible, cameras, tile_lists, tile_blocks, targets):
    own_rows = visible.shape[1]
    owners = views * tiles
    per_device, entries = tile_lists.shape[1:]
    blocks = entries // BLOCK
    block_shape = (SUBS, 2 * own_rows)
    f32 = jnp.float32
    dma = pltpu.SemaphoreType.DMA
    everyone, picked = pl.pallas_call(
        functools.partial(send_kernel, views, tiles),
        out_shape=[
            jax.ShapeDtypeStruct((tiles, views) + block_shape, f32),
            jax.ShapeDtypeStruct((64, views * own_rows), f32),
        ],
        in_specs=[VMEM, VMEM, SMEM],
        out_specs=[VMEM, VMEM],
        scratch_shapes=[
            pltpu.VMEM((views,) + block_shape, f32),
            dma((views,)), dma((views,)), dma((tiles,)), dma((tiles,)),
        ],
        compiler_params=pltpu.CompilerParams(
            collective_id=0, has_side_effects=True, vmem_limit_bytes=LIMIT
        ),
        name="project_send",
    )(params, visible, cameras)
    chunk = min(owners, 32)
    given, rendered = pl.pallas_call(
        functools.partial(composite_kernel, owners, chunk),
        out_shape=[
            jax.ShapeDtypeStruct((owners * SUBS, 2 * own_rows), f32),
            jax.ShapeDtypeStruct((3, per_device * PIX), f32),
        ],
        in_specs=[VMEM, VMEM, SMEM, VMEM],
        out_specs=[VMEM, VMEM],
        scratch_shapes=[
            pltpu.VMEM((per_device, 2 * SUBS, entries), f32),
            pltpu.VMEM((per_device, 2 * SUBS, entries), f32),
            pltpu.VMEM((per_device, blocks, PIX, BLOCK), f32),
            pltpu.VMEM((per_device, blocks, PIX, 2 * BLOCK), jnp.bfloat16),
            pltpu.VMEM((per_device, blocks, PIX, BLOCK), f32),
            pltpu.VMEM((per_device, PIX, BLOCK), f32),
            pltpu.VMEM((per_device, PIX, 2 * SUBS), f32),
        ],
        compiler_params=pltpu.CompilerParams(vmem_limit_bytes=LIMIT),
        name="composite",
    )(everyone.reshape(owners * SUBS, 2 * own_rows), tile_lists[0], tile_blocks, targets[0])
    arrived = pl.pallas_call(
        functools.partial(return_kernel, views, tiles),
        out_shape=jax.ShapeDtypeStruct((views,) + block_shape, f32),
        in_specs=[VMEM],
        out_specs=VMEM,
        scratch_shapes=[
            pltpu.VMEM((tiles, views) + block_shape, f32),
            pltpu.VMEM((views,) + block_shape, f32),
            dma((views,)), dma((views,)), dma((tiles,)), dma((tiles,)),
        ],
        compiler_params=pltpu.CompilerParams(
            collective_id=1, has_side_effects=True, vmem_limit_bytes=LIMIT
        ),
        name="gradient_return",
    )(given.reshape((tiles, views) + block_shape))
    like = jax.ShapeDtypeStruct(params.shape, f32)
    new_params, new_first, new_second = pl.pallas_call(
        update_kernel,
        out_shape=[like, like, like],
        in_specs=[VMEM, VMEM, VMEM, VMEM, SMEM, VMEM, VMEM],
        out_specs=[VMEM, VMEM, VMEM],
        scratch_shapes=[pltpu.VMEM((64, views * own_rows), f32)],
        compiler_params=pltpu.CompilerParams(vmem_limit_bytes=LIMIT),
        name="update",
    )(params, first, second, visible, cameras, picked, arrived)
    return (new_params, new_first, new_second, rendered[None])


def solution(mesh):
    in_specs = (
        P(None, ("view", "tile")),
        P(None, ("view", "tile")),
        P(None, ("view", "tile")),
        P(None, ("view", "tile")),
        P(),
        P("view", "tile", None),
        P("view", "tile"),
        P("view", None, "tile"),
    )
    out_specs = (
        P(None, ("view", "tile")),
        P(None, ("view", "tile")),
        P(None, ("view", "tile")),
        P("view", None, "tile"),
    )
    body = functools.partial(shards, mesh.shape["view"], mesh.shape["tile"])
    return jax.shard_map(body, mesh=mesh, in_specs=in_specs, out_specs=out_specs, check_vma=False)
```

time: 168 us -> 44.9 us (0.27)
  Pallas kernels: 0 us -> 40 us
  matrix products: 31.4 us -> 0 us
  other arithmetic: 31.3 us -> 0 us
  waiting for transfers between devices: 29.8 us -> 0 us
  local copies, waits for them, and re-layouts: 27.5 us -> 3.92 us
  between operations: 14.4 us -> 0.71 us
  loops' own time: 13.1 us -> 0 us
  starting transfers between devices: 11.1 us -> 0 us
  blocking collectives: 8.46 us -> 0 us
    pallas_call x0 -> x4, Pallas kernels: none -> 40 us  [the longest x1 14.8 us: shards(): pl.pallas_call(functools.partial(composite_kernel, owners, chunk), out_sh...]
    dot_general x80 -> x0, matrix products: 31.4 us -> none  [the longest x48 18.1 us: advance(): lax.dot_general(piece[6:9], weight, (((1,), (1,)), ((), ())), precision=l...]
    reduce_scatter x1 -> x0, waiting for transfers between devices: 21.1 us -> none  [shards(): lax.psum_scatter(gathered_grad, 'tile', scatter_dimension=1, tiled=True)]
    scatter-add x3 -> x0, other arithmetic: 18.9 us -> none  [the longest x1 12.5 us: shards(): jnp.zeros(everyone.shape, jnp.float32).at[:, lists.reshape(-1)].add(spread)]
    another operation x1 -> x0, loops' own time: 13.1 us -> none  [shards(): lax.map(one_tile, (jnp.arange(per_device, dtype=jnp.int32), lists, counts...]
    all_to_all x2 -> x0, starting transfers between devices: 11.1 us -> none  [the longest x1 6.46 us: shards(): lax.all_to_all(outgoing, 'view', split_axis=1, concat_axis=1, tiled=True)]
    all_to_all x2 -> x0, waiting for transfers between devices: 8.72 us -> none  [the longest x1 4.86 us: shards(): lax.all_to_all(outgoing, 'view', split_axis=1, concat_axis=1, tiled=True)]
    all_gather x1 -> x0, blocking collectives: 8.46 us -> none  [shards(): everyone = lax.all_gather(projected, 'tile', axis=1, tiled=True)]
  transfers between devices with their start and end apart: 3 -> 0, of which waited for: 3 -> 0; matrix products, arithmetic and copies ran while one was open for 3% -> 0% of each run, Pallas kernels for 0% -> 0%
where the time goes in v1:
time: 44.9 us; the launch traced here: 44.7 us
  Pallas kernels  40 us (89%)
  local copies, waits for them, and re-layouts  3.92 us (9%)
  between operations  0.71 us (2%)
    pallas_call x1, Pallas kernels, shards(): pl.pallas_call(functools.partial(composite_kernel, owners, chunk), out_sh...  14.8 us
    pallas_call x1, Pallas kernels, shards(): pl.pallas_call(functools.partial(send_kernel, views, tiles), out_shape=[j...  12.9 us
    pallas_call x1, Pallas kernels, shards(): pl.pallas_call(functools.partial(return_kernel, views, tiles), out_shape=...  9.75 us
    unnamed x18, local copies, waits for them, and re-layouts  3.92 us
    pallas_call x1, Pallas kernels, shards(): pl.pallas_call(update_kernel, out_shape=[like, like, like], in_specs=[VME...  2.58 us

profile of v1, /device:TPU:0, one launch (start us, length us, event | category | flops | bytes accessed | tf_op | source)
XLA Modules:
  0.0 44.7 jit_solution(12791575523398747653)
XLA Ops:
  0.6 0.0 copy-start.4
  0.6 0.0 copy-start.5
  0.7 0.0 copy-start.7
  0.7 0.7 %copy.15 = f32[1,3,512]{2,1,0:T(4,128)S(1)} copy(f32[1,3,512]{2,0,1:T(1,128)} %param.15) | data formatting | bytes 12288
  1.4 0.0 copy-done.4
  1.4 0.0 copy-done.5
  1.4 0.0 copy-start
  1.4 0.9 %copy-done = f32[59,1024]{1,0:T(8,128)S(1)} copy-done((f32[59,1024]{1,0:T(8,128)S(1)}, f32[59,1024]{1,0:T(8,128)}, u32[]{:S(2)}) %copy-start) | copy-done | bytes 241688
  2.3 0.0 copy-start.1
  2.3 0.0 copy-start.2
  2.3 12.9 %project_send.1 = (f32[4,8,8,128]{3,2,1,0:T(8,128)S(1)}, f32[64,512]{1,0:T(8,128)S(1)}) custom-call(f32[59,1024]{1,0:T(8,128)S(1)} %copy-done, s32[8,64]{1,0:T(8,128)S(1)} %copy-done.4, f32[8,11]{1,0:T(8,128)S(1)} %copy-done.5), custom_call_target="tpu_custom_call" | custom-call | tf_op jit(solution)/shard_map/project_send/pallas_call | solution.py:579
  15.3 0.0 copy-done.7
  15.3 0.0 copy-start.6
  15.3 0.7 %copy-done.6 = s32[1,2,1024]{2,1,0:T(2,128)S(1)} copy-done((s32[1,2,1024]{2,1,0:T(2,128)S(1)}, s32[1,2,1024]{2,1,0:T(2,128)}, u32[]{:S(2)}) %copy-start.6) | copy-done | bytes 8216
  16.0 14.8 %composite.1 = (f32[256,128]{1,0:T(8,128)S(1)}, f32[3,512]{1,0:T(4,128)S(1)}) custom-call(f32[256,128]{1,0:T(8,128)S(1)} %bitcast.8, s32[2,1024]{1,0:T(2,128)S(1)} %bitcast.10, s32[1,2]{1,0:T(1,128)S(1)} %copy-done.7, f32[3,512]{1,0:T(4,128)S(1)} %bitcast.9), custom_call_target="tpu_custom_call" | custom-call | tf_op jit(solution)/shard_map/composite/pallas_call | solution.py:597
  30.8 9.8 %gradient_return.1.arrived_ref = f32[8,8,128]{2,1,0:T(8,128)S(1)} custom-call(f32[4,8,8,128]{3,2,1,0:T(8,128)S(1)} %bitcast.7), custom_call_target="tpu_custom_call" | custom-call | tf_op jit(solution)/shard_map/gradient_return/pallas_call | solution.py:617
  40.5 0.6 %copy.12 = f32[1,3,512]{2,0,1:T(1,128)} copy(f32[1,3,512]{2,1,0:T(4,128)S(1)} %bitcast.11) | data formatting | bytes 12288
  41.1 0.0 copy-done.1
  41.1 0.0 copy-done.2
  41.1 0.0 copy-start.3
  41.1 0.9 %copy-done.3 = f32[59,1024]{1,0:T(8,128)S(1)} copy-done((f32[59,1024]{1,0:T(8,128)S(1)}, f32[59,1024]{1,0:T(8,128)}, u32[]{:S(2)}) %copy-start.3) | copy-done | bytes 241688
  42.1 2.6 %update.1 = (f32[59,1024]{1,0:T(8,128)}, f32[59,1024]{1,0:T(8,128)}, f32[59,1024]{1,0:T(8,128)}) custom-call(f32[59,1024]{1,0:T(8,128)S(1)} %copy-done.1, f32[59,1024]{1,0:T(8,128)S(1)} %copy-done.2, f32[59,1024]{1,0:T(8,128)S(1)} %copy-done.3, s32[8,64]{1,0:T(8,128)S(1)} %copy-done.4, f32[8,11]{1,0:T(8,128)S(1)} %copy-done.5, ...), custom_call_target="tpu_custom_call" | custom-call | tf_op jit(solution)/shard_map/update/pallas_call | solution.py:633
Async XLA Ops:
  0.6 0.7 %copy-start.4 = (s32[8,64]{1,0:T(8,128)S(1)}, s32[8,64]{1,0:T(8,128)}, u32[]{:S(2)}) copy-start(s32[8,64]{1,0:T(8,128)} %visible_ref.3) | copy-start | bytes 6148
  0.6 0.7 %copy-start.5 = (f32[8,11]{1,0:T(8,128)S(1)}, f32[8,11]{1,0:T(8,128)}, u32[]{:S(2)}) copy-start(f32[8,11]{1,0:T(8,128)} %cameras_ref.3) | copy-start | bytes 1060
  0.7 14.6 %copy-start.7 = (s32[1,2]{1,0:T(1,128)S(1)}, s32[1,2]{1,0:T(1,128)}, u32[]{:S(2)}) copy-start(s32[1,2]{1,0:T(1,128)} %counts_ref.1) | copy-start | bytes 28
  1.4 1.0 %copy-start = (f32[59,1024]{1,0:T(8,128)S(1)}, f32[59,1024]{1,0:T(8,128)}, u32[]{:S(2)}) copy-start(f32[59,1024]{1,0:T(8,128)} %params_ref.3) | copy-start | bytes 724996
  2.3 38.8 %copy-start.1 = (f32[59,1024]{1,0:T(8,128)S(1)}, f32[59,1024]{1,0:T(8,128)}, u32[]{:S(2)}) copy-start(f32[59,1024]{1,0:T(8,128)} %params_ref.3) | copy-start | bytes 724996
  2.3 38.8 %copy-start.2 = (f32[59,1024]{1,0:T(8,128)S(1)}, f32[59,1024]{1,0:T(8,128)}, u32[]{:S(2)}) copy-start(f32[59,1024]{1,0:T(8,128)} %first_ref.1) | copy-start | bytes 724996
  15.3 0.7 %copy-start.6 = (s32[1,2,1024]{2,1,0:T(2,128)S(1)}, s32[1,2,1024]{2,1,0:T(2,128)}, u32[]{:S(2)}) copy-start(s32[1,2,1024]{2,1,0:T(2,128)} %param.13) | copy-start | bytes 24580
  41.1 1.0 %copy-start.3 = (f32[59,1024]{1,0:T(8,128)S(1)}, f32[59,1024]{1,0:T(8,128)}, u32[]{:S(2)}) copy-start(f32[59,1024]{1,0:T(8,128)} %second_ref.1) | copy-start | bytes 724996

commit v2 on v1

v2 whole, which is shorter than its diff:
```python
import functools

import jax
import jax.numpy as jnp
from jax import lax
from jax.experimental import pallas as pl
from jax.experimental.pallas import tpu as pltpu
from jax.sharding import PartitionSpec as P

SIDE = 16
PIX = 256
BLOCK = 128
WIN_COLS = 8
SUBS = 8
MESH = pl.DeviceIdType.MESH
VMEM = pl.BlockSpec(memory_space=pltpu.VMEM)
ANY = pl.BlockSpec(memory_space=pl.ANY)
SMEM = pl.BlockSpec(memory_space=pltpu.SMEM)
LIMIT = 48 * 1024 * 1024


harm_zero = 0.28209479177387814
harm_one = 0.4886025119029199
harm_two = (
    1.0925484305920792,
    -1.0925484305920792,
    0.31539156525252005,
    -1.0925484305920792,
    0.5462742152960396,
)
harm_three = (
    -0.5900435899266435,
    2.890611442640554,
    -0.4570457994644658,
    0.3731763325901154,
    -0.4570457994644658,
    1.445305721320277,
    -0.5900435899266435,
)
learn_rate = 0.05
beta_first = 0.9
beta_second = 0.999
adam_eps = 1e-08
blur_add = 0.3


def rotation(real_part, axis_one, axis_two, axis_three):
    inverse = lax.rsqrt(
        real_part * real_part + axis_one * axis_one + axis_two * axis_two + axis_three * axis_three
    )
    real_unit = real_part * inverse
    unit_one = axis_one * inverse
    unit_two = axis_two * inverse
    unit_three = axis_three * inverse
    return (
        (
            1.0 - 2.0 * (unit_two * unit_two + unit_three * unit_three),
            2.0 * (unit_one * unit_two - real_unit * unit_three),
            2.0 * (unit_one * unit_three + real_unit * unit_two),
        ),
        (
            2.0 * (unit_one * unit_two + real_unit * unit_three),
            1.0 - 2.0 * (unit_one * unit_one + unit_three * unit_three),
            2.0 * (unit_two * unit_three - real_unit * unit_one),
        ),
        (
            2.0 * (unit_one * unit_three - real_unit * unit_two),
            2.0 * (unit_two * unit_three + real_unit * unit_one),
            1.0 - 2.0 * (unit_one * unit_one + unit_two * unit_two),
        ),
    )


def harmonics(first_dir, second_dir, third_dir):
    sq_first = first_dir * first_dir
    sq_second = second_dir * second_dir
    sq_third = third_dir * third_dir
    return [
        harm_zero,
        -harm_one * second_dir,
        harm_one * third_dir,
        -harm_one * first_dir,
        harm_two[0] * first_dir * second_dir,
        harm_two[1] * second_dir * third_dir,
        harm_two[2] * (2.0 * sq_third - sq_first - sq_second),
        harm_two[3] * first_dir * third_dir,
        harm_two[4] * (sq_first - sq_second),
        harm_three[0] * second_dir * (3.0 * sq_first - sq_second),
        harm_three[1] * first_dir * second_dir * third_dir,
        harm_three[2] * second_dir * (4.0 * sq_third - sq_first - sq_second),
        harm_three[3] * third_dir * (2.0 * sq_third - 3.0 * sq_first - 3.0 * sq_second),
        harm_three[4] * first_dir * (4.0 * sq_third - sq_first - sq_second),
        harm_three[5] * third_dir * (sq_first - sq_second),
        harm_three[6] * first_dir * (sq_first - 3.0 * sq_second),
    ]


def project(raw, camera):
    camera_turn = rotation(camera[0], camera[1], camera[2], camera[3])
    shift_vec = (camera[4], camera[5], camera[6])
    focal_x = camera[7]
    focal_y = camera[8]
    position = (raw[0], raw[1], raw[2])
    viewed = [
        camera_turn[across][0] * position[0]
        + camera_turn[across][1] * position[1]
        + camera_turn[across][2] * position[2]
        + shift_vec[across]
        for across in range(3)
    ]
    inverse = 1.0 / viewed[2]
    mean_x = focal_x * viewed[0] * inverse + camera[9]
    mean_y = focal_y * viewed[1] * inverse + camera[10]
    gauss_turn = rotation(raw[6], raw[7], raw[8], raw[9])
    stretch = [jnp.exp(raw[3 + column]) for column in range(3)]
    jac_xx = focal_x * inverse
    jac_xz = -focal_x * viewed[0] * inverse * inverse
    jac_yy = focal_y * inverse
    jac_yz = -focal_y * viewed[1] * inverse * inverse
    leading_x = [
        jac_xx * camera_turn[0][column] + jac_xz * camera_turn[2][column] for column in range(3)
    ]
    leading_y = [
        jac_yy * camera_turn[1][column] + jac_yz * camera_turn[2][column] for column in range(3)
    ]
    axes_x = [
        (
            leading_x[0] * gauss_turn[0][column]
            + leading_x[1] * gauss_turn[1][column]
            + leading_x[2] * gauss_turn[2][column]
        )
        * stretch[column]
        for column in range(3)
    ]
    axes_y = [
        (
            leading_y[0] * gauss_turn[0][column]
            + leading_y[1] * gauss_turn[1][column]
            + leading_y[2] * gauss_turn[2][column]
        )
        * stretch[column]
        for column in range(3)
    ]
    cov_xx = axes_x[0] * axes_x[0] + axes_x[1] * axes_x[1] + axes_x[2] * axes_x[2] + blur_add
    cov_xy = axes_x[0] * axes_y[0] + axes_x[1] * axes_y[1] + axes_x[2] * axes_y[2]
    cov_yy = axes_y[0] * axes_y[0] + axes_y[1] * axes_y[1] + axes_y[2] * axes_y[2] + blur_add
    determ = cov_xx * cov_yy - cov_xy * cov_xy
    opacity = 1.0 / (1.0 + jnp.exp(-raw[10]))
    camera_eye = [
        -(
            camera_turn[0][column] * shift_vec[0]
            + camera_turn[1][column] * shift_vec[1]
            + camera_turn[2][column] * shift_vec[2]
        )
        for column in range(3)
    ]
    offset = [position[column] - camera_eye[column] for column in range(3)]
    length = lax.rsqrt(offset[0] * offset[0] + offset[1] * offset[1] + offset[2] * offset[2])
    harmonic_terms = harmonics(offset[0] * length, offset[1] * length, offset[2] * length)
    colours = []
    for channel in range(3):
        total = 0.5 + jnp.zeros_like(opacity)
        for harmonic in range(16):
            total = total + raw[11 + 16 * channel + harmonic] * harmonic_terms[harmonic]
        colours.append(total)
    return [mean_x, mean_y, cov_yy / determ, -cov_xy / determ, cov_xx / determ, opacity] + colours


def three_pieces(value):
    high = value.astype(jnp.bfloat16)
    rest = value - high.astype(jnp.float32)
    middle = rest.astype(jnp.bfloat16)
    low = (rest - middle.astype(jnp.float32)).astype(jnp.bfloat16)
    return high, middle, low


def two_pieces(value):
    high = value.astype(jnp.bfloat16)
    return high, (value - high.astype(jnp.float32)).astype(jnp.bfloat16)


def matmul(left, right):
    return jnp.dot(left, right, preferred_element_type=jnp.float32)


def matmul_nt(left, right):
    return lax.dot_general(
        left, right, (((1,), (1,)), ((), ())), preferred_element_type=jnp.float32
    )


def column_hot(visible_ref, columns):
    views = visible_ref.shape[0]
    ids = jnp.concatenate([visible_ref[view : view + 1, :] for view in range(views)], axis=1)
    place = lax.broadcasted_iota(jnp.int32, (columns, ids.shape[1]), 0)
    return jnp.where(place == ids, 1.0, 0.0).astype(jnp.bfloat16)


def camera_rows(cameras_ref, own_rows):
    views = cameras_ref.shape[0]
    lane = lax.broadcasted_iota(jnp.int32, (1, views * own_rows), 1)
    rows = []
    for entry in range(11):
        row = jnp.full(lane.shape, cameras_ref[0, entry], jnp.float32)
        for view in range(1, views):
            row = jnp.where(lane >= view * own_rows, cameras_ref[view, entry], row)
        rows.append(row)
    return rows


def list_hot(lists, lanes):
    place = lax.broadcasted_iota(jnp.int32, (lanes, lists.shape[1]), 0)
    hot = jnp.where(place == lax.bitwise_and(lists, lanes - 1), 1.0, 0.0).astype(jnp.bfloat16)
    return hot, lax.shift_right_logical(lists, lanes.bit_length() - 1)


def step_kernel(
    views, tiles, params_hbm, visible_ref, cameras_ref, lists_hbm, counts_ref, targets_ref,
    picked_ref, arrived_ref, image_ref,
    params_ref, lists_ref, outgoing, everyone, hots, hots_wide, rows, grads, weights,
    weight_parts, ratios, carried, held, given, landed, summed,
    load_sem, out_sem, out_recv, spread_sem, spread_recv, view_send, view_recv, tile_send, tile_recv
):
    my_view, my_tile = lax.axis_index("view"), lax.axis_index("tile")
    others_view = [lax.rem(my_view + step, views) for step in range(1, views)]
    others_tile = [lax.rem(my_tile + step, tiles) for step in range(1, tiles)]
    barrier = pltpu.get_barrier_semaphore()
    for other in others_view:
        pl.semaphore_signal(barrier, inc=1, device_id=(other, my_tile), device_id_type=MESH)
    for other in others_tile:
        pl.semaphore_signal(barrier, inc=1, device_id=(my_view, other), device_id_type=MESH)
    load_params = pltpu.make_async_copy(params_hbm, params_ref, load_sem.at[0])
    load_lists = pltpu.make_async_copy(lists_hbm, lists_ref, load_sem.at[1])
    load_params.start()
    load_lists.start()

    width, columns = params_ref.shape
    own_rows = visible_ref.shape[1]
    wide = 2 * own_rows
    hot = column_hot(visible_ref, columns)
    cameras = camera_rows(cameras_ref, own_rows)
    load_params.wait()
    padded = jnp.concatenate(
        [params_ref[...], jnp.zeros((64 - width, columns), jnp.float32)], axis=0
    )
    found = matmul(jnp.concatenate(three_pieces(padded), axis=0), hot)
    picked_ref[...] = found[0:64] + found[64:128] + found[128:192]
    raw = [picked_ref[row : row + 1, :] for row in range(width)]
    out = project(raw, cameras)
    lower = jnp.concatenate(out[0:8], axis=0)
    upper = jnp.concatenate([out[8], jnp.zeros((7, out[8].shape[1]), jnp.float32)], axis=0)
    for view in range(views):
        span = slice(view * own_rows, (view + 1) * own_rows)
        outgoing[view] = jnp.concatenate([lower[:, span], upper[:, span]], axis=1)

    def to_view(source, other, landing, sends, receives, slot):
        return pltpu.make_async_remote_copy(
            src_ref=source.at[other], dst_ref=landing, send_sem=sends.at[other],
            recv_sem=receives.at[slot], device_id=(other, my_tile), device_id_type=MESH,
        )

    def spread(place, view, other, slot):
        return pltpu.make_async_remote_copy(
            src_ref=everyone.at[my_tile, view], dst_ref=everyone.at[place, view],
            send_sem=spread_sem.at[other, view], recv_sem=spread_recv.at[slot, view],
            device_id=(my_view, other), device_id_type=MESH,
        )

    everyone[my_tile, my_view] = outgoing[my_view]
    pl.semaphore_wait(barrier, views + tiles - 2)
    for other in others_view:
        to_view(outgoing, other, everyone.at[my_tile, my_view], out_sem, out_recv, my_view).start()
    for other in others_tile:
        spread(my_tile, my_view, other, my_tile).start()

    load_lists.wait()
    per_device, entries = lists_ref.shape
    groups, groups_wide = [], []
    for tile in range(per_device):
        ids = lists_ref[tile : tile + 1, :]
        narrow, group = list_hot(ids, own_rows)
        hots[tile] = jnp.concatenate([narrow] * 4, axis=0)
        groups.append(jnp.broadcast_to(group, (SUBS, entries)))
        hots_wide[tile], group = list_hot(ids, wide)
        groups_wide.append(jnp.broadcast_to(group, (SUBS, entries)))

    for other in others_view:
        to_view(outgoing, other, everyone.at[my_tile, other], out_sem, out_recv, other).wait_recv()
        for peer in others_tile:
            spread(my_tile, other, peer, my_tile).start()
    for other in others_view:
        to_view(outgoing, other, everyone.at[my_tile, my_view], out_sem, out_recv, my_view).wait_send()
    for peer in others_tile:
        for view in range(views):
            copy = spread(peer, view, peer, peer)
            copy.wait_send()
            copy.wait_recv()

    batch = max(1, min(tiles, 32 // views))
    chunk = batch * views
    lane = lax.broadcasted_iota(jnp.int32, (chunk * (SUBS + 1), wide), 1)

    def gather(index, held_rows):
        source = everyone[pl.ds(index * batch, batch)].reshape(chunk, SUBS, wide)
        last = pltpu.roll(source[:, 0, :], own_rows, 1)
        source = jnp.concatenate([source.reshape(chunk * SUBS, wide), last], axis=0)
        high, middle, low = [piece.astype(jnp.float32) for piece in three_pieces(source)]
        source = jnp.concatenate(
            [
                jnp.where(lane < own_rows, high, pltpu.roll(middle, own_rows, 1)),
                jnp.where(lane < own_rows, low, 0.0),
            ],
            axis=1,
        ).astype(jnp.bfloat16)
        new_rows = []
        for tile in range(per_device):
            located = matmul(source, hots[tile])
            first, second = held_rows[tile]
            for owner in range(chunk):
                mine = groups[tile] == index * chunk + owner
                first = first + jnp.where(mine, located[owner * SUBS : (owner + 1) * SUBS], 0.0)
            for start in range(0, chunk, SUBS):
                begin = chunk * SUBS + start
                number = lax.broadcasted_iota(jnp.int32, (SUBS, entries), 0) + (
                    index * chunk + start
                )
                second = second + jnp.where(
                    groups[tile] == number, located[begin : begin + SUBS], 0.0
                )
            new_rows.append((first, second))
        return tuple(new_rows)

    empty = jnp.zeros((SUBS, entries), jnp.float32)
    collected = lax.fori_loop(0, tiles // batch, gather, ((empty, empty),) * per_device)
    for tile in range(per_device):
        rows[tile, 0:SUBS, :] = collected[tile][0]
        rows[tile, SUBS : 2 * SUBS, :] = jnp.broadcast_to(
            jnp.sum(collected[tile][1], axis=0, keepdims=True), (SUBS, entries)
        )

    first_tile = my_tile * per_device
    half = SIDE // 2
    middles = []
    for tile in range(per_device):
        number = first_tile + tile
        middles.append(
            (
                (lax.rem(number, WIN_COLS) * SIDE + half).astype(jnp.float32),
                (lax.div(number, WIN_COLS) * SIDE + half).astype(jnp.float32),
            )
        )
    side_x = lax.broadcasted_iota(jnp.int32, (SIDE, BLOCK), 0).astype(jnp.float32) + (0.5 - half)
    spot = lax.bitwise_and(
        lax.broadcasted_iota(jnp.int32, (2 * BLOCK, 2 * BLOCK), 0), BLOCK - 1
    )
    lane_two = lax.broadcasted_iota(jnp.int32, (2 * BLOCK, 2 * BLOCK), 1)
    ahead = jnp.where((spot < lane_two) | (lane_two >= BLOCK), 1.0, 0.0).astype(jnp.bfloat16)
    behind = jnp.where((spot > lane_two) | (lane_two >= BLOCK), 1.0, 0.0).astype(jnp.bfloat16)
    blocks = entries // BLOCK

    carried[...] = jnp.zeros_like(carried)
    held[...] = jnp.zeros_like(held)

    def forward(block, _):
        start = pl.multiple_of(block * BLOCK, BLOCK)
        for tile in range(per_device):
            live = (block < counts_ref[0, tile]).astype(jnp.float32)
            low = rows[tile, 0:SUBS, pl.ds(start, BLOCK)]
            up = rows[tile, SUBS : 2 * SUBS, pl.ds(start, BLOCK)]
            mean_x = low[0:1] - middles[tile][0]
            mean_y = low[1:2] - middles[tile][1]
            form_a = -0.5 * low[2:3]
            form_b = -low[3:4]
            form_c = -0.5 * low[4:5]
            opacity = low[5:6] * live
            delta_x = side_x - mean_x
            square = form_a * delta_x * delta_x
            cross = form_b * delta_x
            pieces = []
            for line in range(SIDE):
                delta_y = (line + 0.5 - half) - mean_y
                pieces.append((cross + form_c * delta_y) * delta_y + square)
            alpha = opacity * jnp.exp(jnp.concatenate(pieces, axis=0))
            decay = jnp.log(1.0 - alpha)
            before = matmul(jnp.concatenate(two_pieces(decay), axis=1), ahead)
            past = carried[tile]
            weight = alpha * jnp.exp(before[:, 0:BLOCK] + past)
            carried[tile] = past + before[:, BLOCK:]
            ratios[tile, block] = alpha * jnp.exp(-decay)
            weights[tile, block] = weight
            parts = jnp.concatenate(two_pieces(weight), axis=1)
            weight_parts[tile, block] = parts
            colour = jnp.concatenate([low[6:8], up[0:1], jnp.zeros((5, BLOCK), jnp.float32)], axis=0)
            high = colour.astype(jnp.bfloat16).astype(jnp.float32)
            both = jnp.concatenate([high, colour - high], axis=0).astype(jnp.bfloat16)
            held[tile] += matmul_nt(parts, jnp.concatenate([both, both], axis=1))
        return 0

    lax.fori_loop(0, blocks, forward, 0)

    slopes, slopes_wide = [], []
    for tile in range(per_device):
        drawn = jnp.transpose(
            jnp.concatenate(
                [held[tile], jnp.zeros((PIX, BLOCK - 2 * SUBS), jnp.float32)], axis=1
            )
        )
        drawn = drawn[0:3] + drawn[SUBS : SUBS + 3]
        image_ref[:, 0, tile * PIX : (tile + 1) * PIX] = drawn
        slope = 2.0 * (drawn - targets_ref[:, 0, tile * PIX : (tile + 1) * PIX])
        high = slope.astype(jnp.bfloat16).astype(jnp.float32)
        stack = jnp.concatenate(
            [high, slope - high, high, jnp.zeros((BLOCK - 9, PIX), jnp.float32)], axis=0
        )
        slopes.append(stack[0 : 2 * SUBS].astype(jnp.bfloat16))
        slopes_wide.append(jnp.transpose(stack).astype(jnp.bfloat16)[:, 0 : 2 * SUBS])

    pixel = lax.broadcasted_iota(jnp.int32, (2 * SUBS, PIX), 1)
    kind = lax.broadcasted_iota(jnp.int32, (2 * SUBS, PIX), 0)
    at_x = lax.bitwise_and(pixel, SIDE - 1).astype(jnp.float32) + (0.5 - half)
    at_y = lax.shift_right_logical(pixel, SIDE.bit_length() - 1).astype(jnp.float32) + (0.5 - half)
    power_x = jnp.where((kind == 1) | (kind == 4), at_x, jnp.where(kind == 3, at_x * at_x, 1.0))
    power_y = jnp.where((kind == 2) | (kind == 4), at_y, jnp.where(kind == 5, at_y * at_y, 1.0))
    basis = jnp.where(kind < 6, power_x * power_y, 0.0).astype(jnp.bfloat16)

    carried[...] = jnp.zeros_like(carried)

    def backward(index, _):
        block = blocks - 1 - index
        start = pl.multiple_of(block * BLOCK, BLOCK)
        for tile in range(per_device):
            low = rows[tile, 0:SUBS, pl.ds(start, BLOCK)]
            up = rows[tile, SUBS : 2 * SUBS, pl.ds(start, BLOCK)]
            colour = jnp.concatenate([low[6:8], up[0:1]], axis=0)
            high = colour.astype(jnp.bfloat16).astype(jnp.float32)
            both = jnp.concatenate(
                [high, high, colour - high, jnp.zeros((7, BLOCK), jnp.float32)], axis=0
            ).astype(jnp.bfloat16)
            pulled = matmul(slopes_wide[tile], both) * weights[tile, block]
            after = matmul(jnp.concatenate(two_pieces(pulled), axis=1), behind)
            past = carried[tile]
            inner = pulled - (after[:, 0:BLOCK] + past) * ratios[tile, block]
            carried[tile] = past + after[:, BLOCK:]
            inner_high, inner_low = two_pieces(inner)
            sums = matmul(basis, inner_high) + matmul(basis, inner_low)
            parts = weight_parts[tile, block]
            tint = matmul(slopes[tile], parts[:, 0:BLOCK])
            tint_low = matmul(slopes[tile], parts[:, BLOCK:])
            tint = tint[0:3] + tint[3:6] + tint_low[0:3]
            mean_x = low[0:1] - middles[tile][0]
            mean_y = low[1:2] - middles[tile][1]
            form_a, form_b, form_c = low[2:3], low[3:4], low[4:5]
            whole, by_x, by_y = sums[0:1], sums[1:2], sums[2:3]
            sum_x = by_x - mean_x * whole
            sum_y = by_y - mean_y * whole
            sum_xx = sums[3:4] - 2.0 * mean_x * by_x + mean_x * mean_x * whole
            sum_xy = sums[4:5] - mean_x * by_y - mean_y * by_x + mean_x * mean_y * whole
            sum_yy = sums[5:6] - 2.0 * mean_y * by_y + mean_y * mean_y * whole
            grads[tile, 0:SUBS, pl.ds(start, BLOCK)] = jnp.concatenate(
                [
                    form_a * sum_x + form_b * sum_y,
                    form_b * sum_x + form_c * sum_y,
                    -0.5 * sum_xx,
                    -sum_xy,
                    -0.5 * sum_yy,
                    whole / low[5:6],
                    tint[0:2],
                ],
                axis=0,
            )
            grads[tile, SUBS : 2 * SUBS, pl.ds(start, BLOCK)] = jnp.broadcast_to(
                tint[2:3], (SUBS, BLOCK)
            )
        return 0

    lax.fori_loop(0, blocks, backward, 0)

    pairs = chunk // 2
    lane_pair = lax.broadcasted_iota(jnp.int32, (pairs, SUBS, wide), 2)

    def scatter(index, _):
        total = jnp.zeros((2 * pairs * (SUBS + 1), wide), jnp.float32)
        for tile in range(per_device):
            main = grads[tile, 0:SUBS, :]
            last = grads[tile, SUBS : 2 * SUBS, :]
            parts = [[], [], [], []]
            main_high = main.astype(jnp.bfloat16).astype(jnp.float32)
            last_high = last.astype(jnp.bfloat16).astype(jnp.float32)
            for pair in range(pairs):
                mine = groups_wide[tile] == index * pairs + pair
                parts[0].append(jnp.where(mine, main_high, 0.0))
                parts[1].append(jnp.where(mine, main - main_high, 0.0))
            for start in range(0, pairs, SUBS):
                number = lax.broadcasted_iota(jnp.int32, (SUBS, entries), 0) + (
                    index * pairs + start
                )
                mine = groups_wide[tile] == number
                parts[2].append(jnp.where(mine, last_high, 0.0))
                parts[3].append(jnp.where(mine, last - last_high, 0.0))
            left = jnp.concatenate(parts[0] + parts[1] + parts[2] + parts[3], axis=0)
            total = total + matmul_nt(left.astype(jnp.bfloat16), hots_wide[tile])
        size = pairs * SUBS
        main = (total[0:size] + total[size : 2 * size]).reshape(pairs, SUBS, wide)
        last = total[2 * size : 2 * size + pairs] + total[2 * size + pairs :]
        turned = pltpu.roll(last, own_rows, 1)
        even = jnp.where(
            lane_pair < own_rows, main, jnp.broadcast_to(turned[:, None, :], main.shape)
        )
        odd = jnp.where(
            lane_pair < own_rows,
            pltpu.roll(main, own_rows, 2),
            jnp.broadcast_to(last[:, None, :], main.shape),
        )
        for pair in range(pairs):
            place = index * batch + 2 * pair // views
            given[place, 2 * pair % views] = even[pair]
            given[place, 2 * pair % views + 1] = odd[pair]
        return 0

    lax.fori_loop(0, tiles // batch, scatter, 0)

    def to_tile(other, place, slot):
        return pltpu.make_async_remote_copy(
            src_ref=given.at[other], dst_ref=landed.at[place], send_sem=tile_send.at[other],
            recv_sem=tile_recv.at[slot], device_id=(my_view, other), device_id_type=MESH,
        )

    for other in others_tile:
        to_tile(other, my_tile, my_tile).start()
    total = given[my_tile]
    for other in others_tile:
        to_tile(other, other, other).wait_recv()
        total = total + landed[other]
    summed[...] = total
    for other in others_view:
        to_view(summed, other, arrived_ref.at[my_view], view_send, view_recv, my_view).start()
    arrived_ref[my_view] = summed[my_view]
    for other in others_tile:
        to_tile(other, my_tile, my_tile).wait_send()
    for other in others_view:
        copy = to_view(summed, other, arrived_ref.at[other], view_send, view_recv, other)
        copy.wait_send()
        copy.wait_recv()


def update_kernel(
    params_hbm, first_hbm, second_hbm, visible_ref, cameras_ref, picked_ref, arrived_ref, drawn_ref,
    new_params_hbm, new_first_hbm, new_second_hbm, image_ref,
    params_ref, first_ref, second_ref, new_params, new_first, new_second, slopes, load_sem, store_sem
):
    loads = [
        pltpu.make_async_copy(params_hbm, params_ref, load_sem.at[0]),
        pltpu.make_async_copy(first_hbm, first_ref, load_sem.at[1]),
        pltpu.make_async_copy(second_hbm, second_ref, load_sem.at[2]),
    ]
    for load in loads:
        load.start()
    image_ref[...] = drawn_ref[...]
    width, columns = params_ref.shape
    views, own_rows = visible_ref.shape
    lower = jnp.concatenate([arrived_ref[view][:, 0:own_rows] for view in range(views)], axis=1)
    upper = jnp.concatenate([arrived_ref[view][:, own_rows:] for view in range(views)], axis=1)
    cotangent = [lower[row : row + 1] for row in range(8)] + [upper[0:1]]
    cameras = camera_rows(cameras_ref, own_rows)
    raw = [picked_ref[row : row + 1, :] for row in range(width)]
    _, pullback = jax.vjp(lambda source: project(source, cameras), raw)
    (returned,) = pullback(cotangent)
    slopes[...] = jnp.ones_like(slopes)
    for row in range(width):
        slopes[row : row + 1, :] = returned[row]
    hot = column_hot(visible_ref, columns)
    parts = matmul_nt(jnp.concatenate(three_pieces(slopes[...]), axis=0), hot)
    grad = parts[0:64] + parts[64:128] + parts[128:192]
    seen = grad[width : width + 1] > 0.5
    grad = grad[0:width]
    for load in loads:
        load.wait()
    first, second, params = first_ref[...], second_ref[...], params_ref[...]
    moved_first = beta_first * first + (1.0 - beta_first) * grad
    moved_second = beta_second * second + (1.0 - beta_second) * grad * grad
    new_first[...] = jnp.where(seen, moved_first, first)
    store_first = pltpu.make_async_copy(new_first, new_first_hbm, store_sem.at[1])
    store_first.start()
    new_second[...] = jnp.where(seen, moved_second, second)
    store_second = pltpu.make_async_copy(new_second, new_second_hbm, store_sem.at[2])
    store_second.start()
    moved_params = params - learn_rate * moved_first / (jnp.sqrt(moved_second) + adam_eps)
    new_params[...] = jnp.where(seen, moved_params, params)
    store_params = pltpu.make_async_copy(new_params, new_params_hbm, store_sem.at[0])
    store_params.start()
    store_first.wait()
    store_second.wait()
    store_params.wait()


def shards(views, tiles, params, first, second, visible, cameras, tile_lists, tile_blocks, targets):
    own_rows = visible.shape[1]
    per_device, entries = tile_lists.shape[1:]
    blocks = entries // BLOCK
    packet = (SUBS, 2 * own_rows)
    f32 = jnp.float32
    dma = pltpu.SemaphoreType.DMA
    image_shape = jax.ShapeDtypeStruct((3, 1, per_device * PIX), f32)
    picked, arrived, drawn = pl.pallas_call(
        functools.partial(step_kernel, views, tiles),
        out_shape=[
            jax.ShapeDtypeStruct((64, views * own_rows), f32),
            jax.ShapeDtypeStruct((views,) + packet, f32),
            image_shape,
        ],
        in_specs=[ANY, VMEM, SMEM, ANY, SMEM, VMEM],
        out_specs=[VMEM, VMEM, VMEM],
        scratch_shapes=[
            pltpu.VMEM(params.shape, f32),
            pltpu.VMEM((per_device, entries), jnp.int32),
            pltpu.VMEM((views,) + packet, f32),
            pltpu.VMEM((tiles, views) + packet, f32),
            pltpu.VMEM((per_device, 4 * own_rows, entries), jnp.bfloat16),
            pltpu.VMEM((per_device, 2 * own_rows, entries), jnp.bfloat16),
            pltpu.VMEM((per_device, 2 * SUBS, entries), f32),
            pltpu.VMEM((per_device, 2 * SUBS, entries), f32),
            pltpu.VMEM((per_device, blocks, PIX, BLOCK), f32),
            pltpu.VMEM((per_device, blocks, PIX, 2 * BLOCK), jnp.bfloat16),
            pltpu.VMEM((per_device, blocks, PIX, BLOCK), f32),
            pltpu.VMEM((per_device, PIX, BLOCK), f32),
            pltpu.VMEM((per_device, PIX, 2 * SUBS), f32),
            pltpu.VMEM((tiles, views) + packet, f32),
            pltpu.VMEM((tiles, views) + packet, f32),
            pltpu.VMEM((views,) + packet, f32),
            dma((2,)),
            dma((views,)), dma((views,)), dma((tiles, views)), dma((tiles, views)),
            dma((views,)), dma((views,)), dma((tiles,)), dma((tiles,)),
        ],
        compiler_params=pltpu.CompilerParams(
            collective_id=0, has_side_effects=True, vmem_limit_bytes=LIMIT
        ),
        name="render_step",
    )(params, visible, cameras, tile_lists[0], tile_blocks, jnp.transpose(targets, (1, 0, 2)))
    like = jax.ShapeDtypeStruct(params.shape, f32)
    new_params, new_first, new_second, rendered = pl.pallas_call(
        update_kernel,
        out_shape=[like, like, like, image_shape],
        in_specs=[ANY, ANY, ANY, VMEM, SMEM, VMEM, VMEM, VMEM],
        out_specs=[ANY, ANY, ANY, VMEM],
        scratch_shapes=[pltpu.VMEM(params.shape, f32)] * 6
        + [pltpu.VMEM((64, views * own_rows), f32), dma((3,)), dma((3,))],
        compiler_params=pltpu.CompilerParams(vmem_limit_bytes=LIMIT),
        name="update",
    )(params, first, second, visible, cameras, picked, arrived, drawn)
    return (new_params, new_first, new_second, jnp.transpose(rendered, (1, 0, 2)))


def solution(mesh):
    in_specs = (
        P(None, ("view", "tile")),
        P(None, ("view", "tile")),
        P(None, ("view", "tile")),
        P(None, ("view", "tile")),
        P(),
        P("view", "tile", None),
        P("view", "tile"),
        P("view", None, "tile"),
    )
    out_specs = (
        P(None, ("view", "tile")),
        P(None, ("view", "tile")),
        P(None, ("view", "tile")),
        P("view", None, "tile"),
    )
    body = functools.partial(shards, mesh.shape["view"], mesh.shape["tile"])
    return jax.shard_map(body, mesh=mesh, in_specs=in_specs, out_specs=out_specs, check_vma=False)
```

time: 44.9 us -> 43.4 us (0.967)
  Pallas kernels: 40 us -> 37.1 us
  local copies, waits for them, and re-layouts: 3.92 us -> 5.31 us
    pallas_call x4 -> x2, Pallas kernels: 40 us -> 37.1 us  [the longest x1 33.9 us: shards(): pl.pallas_call(functools.partial(step_kernel, views, tiles), out_shape=[j...]
    unnamed x18 -> x16, local copies, waits for them, and re-layouts: 3.92 us -> 5.31 us
where the time goes in v2:
time: 43.4 us; the launch traced here: 43 us
  Pallas kernels  37.1 us (85%)
  local copies, waits for them, and re-layouts  5.31 us (12%)
  between operations  0.67 us (2%)
    pallas_call x1, Pallas kernels, shards(): pl.pallas_call(functools.partial(step_kernel, views, tiles), out_shape=[j...  33.9 us
    unnamed x16, local copies, waits for them, and re-layouts  5.31 us
    pallas_call x1, Pallas kernels, shards(): pl.pallas_call(update_kernel, out_shape=[like, like, like, image_shape],...  3.21 us

profile of v2, /device:TPU:0, one launch (start us, length us, event | category | flops | bytes accessed | tf_op | source)
XLA Modules:
  0.0 43.0 jit_solution(3829751401342661731)
XLA Ops:
  0.6 0.0 copy-start.7
  0.6 0.6 %copy-done.7 = s32[1,2]{1,0:T(1,128)S(1)} copy-done((s32[1,2]{1,0:T(1,128)S(1)}, s32[1,2]{1,0:T(1,128)}, u32[]{:S(2)}) %copy-start.7) | copy-done | bytes 32
  1.3 0.0 copy-start
  1.3 0.9 %copy-done = f32[59,1024]{1,0:T(8,128)S(1)} copy-done((f32[59,1024]{1,0:T(8,128)S(1)}, f32[59,1024]{1,0:T(8,128)}, u32[]{:S(2)}) %copy-start) | copy-done | bytes 241688
  2.2 0.0 copy-start.3
  2.2 0.7 %copy-done.3 = s32[8,64]{1,0:T(8,128)S(1)} copy-done((s32[8,64]{1,0:T(8,128)S(1)}, s32[8,64]{1,0:T(8,128)}, u32[]{:S(2)}) %copy-start.3) | copy-done | bytes 2072
  2.9 0.0 copy-start.4
  2.9 0.7 %copy-done.4 = f32[8,11]{1,0:T(8,128)S(1)} copy-done((f32[8,11]{1,0:T(8,128)S(1)}, f32[8,11]{1,0:T(8,128)}, u32[]{:S(2)}) %copy-start.4) | copy-done | bytes 376
  3.6 0.0 copy-start.5
  3.6 0.7 %copy-done.5 = s32[1,2,1024]{2,1,0:T(2,128)S(1)} copy-done((s32[1,2,1024]{2,1,0:T(2,128)S(1)}, s32[1,2,1024]{2,1,0:T(2,128)}, u32[]{:S(2)}) %copy-start.5) | copy-done | bytes 8216
  4.3 0.0 copy-start.6
  4.3 0.7 %copy-done.6 = f32[1,3,512]{2,0,1:T(1,128)S(1)} copy-done((f32[1,3,512]{2,0,1:T(1,128)S(1)}, f32[1,3,512]{2,0,1:T(1,128)}, u32[]{:S(2)}) %copy-start.6) | copy-done | bytes 6168
  5.0 0.0 copy-start.1
  5.0 33.9 %render_step.1 = (f32[64,512]{1,0:T(8,128)S(1)}, f32[8,8,128]{2,1,0:T(8,128)S(1)}, f32[3,1,512]{2,1,0:T(1,128)S(1)}) custom-call(f32[59,1024]{1,0:T(8,128)S(1)} %copy-done, s32[8,64]{1,0:T(8,128)S(1)} %copy-done.3, f32[8,11]{1,0:T(8,128)S(1)} %copy-done.4, s32[2,1024]{1,0:T(2,128)S(1)} %bitcast.3, s32[1,2]{1,0:T(1,128)S(1)} %copy-done.7, ...), custom_call_target="tpu_custom_call" | custom-call | tf_op jit(solution)/shard_map/render_step/pallas_call | solution.py:604
  38.9 0.0 copy-done.1
  38.9 0.0 copy-start.2
  38.9 0.9 %copy-done.2 = f32[59,1024]{1,0:T(8,128)S(1)} copy-done((f32[59,1024]{1,0:T(8,128)S(1)}, f32[59,1024]{1,0:T(8,128)}, u32[]{:S(2)}) %copy-start.2) | copy-done | bytes 241688
  39.8 3.2 %update.1 = (f32[59,1024]{1,0:T(8,128)}, f32[59,1024]{1,0:T(8,128)}, f32[59,1024]{1,0:T(8,128)}, f32[3,1,512]{2,1,0:T(1,128)}) custom-call(f32[59,1024]{1,0:T(8,128)S(1)} %copy-done, f32[59,1024]{1,0:T(8,128)S(1)} %copy-done.1, f32[59,1024]{1,0:T(8,128)S(1)} %copy-done.2, s32[8,64]{1,0:T(8,128)S(1)} %copy-done.3, f32[8,11]{1,0:T(8,128)S(1)} %copy-done.4, ...), custom_call_target="tpu_custom_call" | custom-call | tf_op jit(solution)/shard_map/update/pallas_call | solution.py:640
Async XLA Ops:
  0.6 0.7 %copy-start.7 = (s32[1,2]{1,0:T(1,128)S(1)}, s32[1,2]{1,0:T(1,128)}, u32[]{:S(2)}) copy-start(s32[1,2]{1,0:T(1,128)} %counts_ref.1) | copy-start | bytes 28
  1.3 0.9 %copy-start = (f32[59,1024]{1,0:T(8,128)S(1)}, f32[59,1024]{1,0:T(8,128)}, u32[]{:S(2)}) copy-start(f32[59,1024]{1,0:T(8,128)} %params_hbm.3) | copy-start | bytes 724996
  2.2 0.7 %copy-start.3 = (s32[8,64]{1,0:T(8,128)S(1)}, s32[8,64]{1,0:T(8,128)}, u32[]{:S(2)}) copy-start(s32[8,64]{1,0:T(8,128)} %visible_ref.3) | copy-start | bytes 6148
  2.9 0.7 %copy-start.4 = (f32[8,11]{1,0:T(8,128)S(1)}, f32[8,11]{1,0:T(8,128)}, u32[]{:S(2)}) copy-start(f32[8,11]{1,0:T(8,128)} %cameras_ref.3) | copy-start | bytes 1060
  3.6 0.7 %copy-start.5 = (s32[1,2,1024]{2,1,0:T(2,128)S(1)}, s32[1,2,1024]{2,1,0:T(2,128)}, u32[]{:S(2)}) copy-start(s32[1,2,1024]{2,1,0:T(2,128)} %param.13) | copy-start | bytes 24580
  4.3 0.7 %copy-start.6 = (f32[1,3,512]{2,0,1:T(1,128)S(1)}, f32[1,3,512]{2,0,1:T(1,128)}, u32[]{:S(2)}) copy-start(f32[1,3,512]{2,0,1:T(1,128)} %param.15) | copy-start | bytes 18436
  5.0 33.9 %copy-start.1 = (f32[59,1024]{1,0:T(8,128)S(1)}, f32[59,1024]{1,0:T(8,128)}, u32[]{:S(2)}) copy-start(f32[59,1024]{1,0:T(8,128)} %first_hbm.1) | copy-start | bytes 724996
  38.9 1.0 %copy-start.2 = (f32[59,1024]{1,0:T(8,128)S(1)}, f32[59,1024]{1,0:T(8,128)}, u32[]{:S(2)}) copy-start(f32[59,1024]{1,0:T(8,128)} %second_hbm.1) | copy-start | bytes 724996

commit v3 on v2

--- a/solution.py
+++ b/solution.py
@@ -16,7 +16,7 @@
 VMEM = pl.BlockSpec(memory_space=pltpu.VMEM)
 ANY = pl.BlockSpec(memory_space=pl.ANY)
 SMEM = pl.BlockSpec(memory_space=pltpu.SMEM)
-LIMIT = 48 * 1024 * 1024
+LIMIT = 62 * 1024 * 1024
 
 
 harm_zero = 0.28209479177387814
@@ -189,9 +189,13 @@
     )
 
 
+def visible_row(visible_ref):
+    views = visible_ref.shape[0]
+    return jnp.concatenate([visible_ref[view : view + 1, :] for view in range(views)], axis=1)
+
+
 def column_hot(visible_ref, columns):
-    views = visible_ref.shape[0]
-    ids = jnp.concatenate([visible_ref[view : view + 1, :] for view in range(views)], axis=1)
+    ids = visible_row(visible_ref)
     place = lax.broadcasted_iota(jnp.int32, (columns, ids.shape[1]), 0)
     return jnp.where(place == ids, 1.0, 0.0).astype(jnp.bfloat16)
 
@@ -208,6 +212,17 @@
     return rows
 
 
+def down(row, lanes):
+    spread_row = jnp.broadcast_to(row.astype(jnp.float32), (lanes, row.shape[1]))
+    return jnp.transpose(spread_row)
+
+
+def list_hot_down(lists, lanes):
+    ids = down(lax.bitwise_and(lists, lanes - 1), lanes)
+    lane = lax.broadcasted_iota(jnp.int32, ids.shape, 1).astype(jnp.float32)
+    return jnp.where(ids == lane, 1.0, 0.0).astype(jnp.bfloat16)
+
+
 def list_hot(lists, lanes):
     place = lax.broadcasted_iota(jnp.int32, (lanes, lists.shape[1]), 0)
     hot = jnp.where(place == lax.bitwise_and(lists, lanes - 1), 1.0, 0.0).astype(jnp.bfloat16)
@@ -216,9 +231,9 @@
 
 def step_kernel(
     views, tiles, params_hbm, visible_ref, cameras_ref, lists_hbm, counts_ref, targets_ref,
-    picked_ref, arrived_ref, image_ref,
-    params_ref, lists_ref, outgoing, everyone, hots, hots_wide, rows, grads, weights,
-    weight_parts, ratios, carried, held, given, landed, summed,
+    grad_ref, seen_ref, image_ref,
+    params_ref, lists_ref, picked_ref, outgoing, everyone, hot_back, hots, hots_wide, rows, grads,
+    weights, weight_parts, ratios, carried, held, given, landed, summed, arrived_ref, slopes_ref,
     load_sem, out_sem, out_recv, spread_sem, spread_recv, view_send, view_recv, tile_send, tile_recv
 ):
     my_view, my_tile = lax.axis_index("view"), lax.axis_index("tile")
@@ -253,25 +268,27 @@
         span = slice(view * own_rows, (view + 1) * own_rows)
         outgoing[view] = jnp.concatenate([lower[:, span], upper[:, span]], axis=1)
 
-    def to_view(source, other, landing, sends, receives, slot):
+    def to_view(source, other, landing, sends, receives):
         return pltpu.make_async_remote_copy(
-            src_ref=source.at[other], dst_ref=landing, send_sem=sends.at[other],
-            recv_sem=receives.at[slot], device_id=(other, my_tile), device_id_type=MESH,
-        )
-
-    def spread(place, view, other, slot):
+            src_ref=source, dst_ref=landing, send_sem=sends, recv_sem=receives,
+            device_id=(other, my_tile), device_id_type=MESH,
+        )
+
+    def spread(source, other, slot):
         return pltpu.make_async_remote_copy(
-            src_ref=everyone.at[my_tile, view], dst_ref=everyone.at[place, view],
-            send_sem=spread_sem.at[other, view], recv_sem=spread_recv.at[slot, view],
-            device_id=(my_view, other), device_id_type=MESH,
+            src_ref=source, dst_ref=source, send_sem=spread_sem.at[other],
+            recv_sem=spread_recv.at[slot], device_id=(my_view, other), device_id_type=MESH,
         )
 
     everyone[my_tile, my_view] = outgoing[my_view]
     pl.semaphore_wait(barrier, views + tiles - 2)
     for other in others_view:
-        to_view(outgoing, other, everyone.at[my_tile, my_view], out_sem, out_recv, my_view).start()
+        to_view(
+            outgoing.at[other], other, everyone.at[my_tile, my_view], out_sem.at[0],
+            out_recv.at[my_view],
+        ).start()
     for other in others_tile:
-        spread(my_tile, my_view, other, my_tile).start()
+        spread(everyone.at[my_tile, my_view], other, my_tile).start()
 
     load_lists.wait()
     per_device, entries = lists_ref.shape
@@ -281,20 +298,25 @@
         narrow, group = list_hot(ids, own_rows)
         hots[tile] = jnp.concatenate([narrow] * 4, axis=0)
         groups.append(jnp.broadcast_to(group, (SUBS, entries)))
-        hots_wide[tile], group = list_hot(ids, wide)
+        hots_wide[tile] = list_hot_down(ids, wide)
+        group = lax.shift_right_logical(ids, wide.bit_length() - 1)
         groups_wide.append(jnp.broadcast_to(group, (SUBS, entries)))
 
     for other in others_view:
-        to_view(outgoing, other, everyone.at[my_tile, other], out_sem, out_recv, other).wait_recv()
+        to_view(
+            outgoing.at[other], other, everyone.at[my_tile, other], out_sem.at[0],
+            out_recv.at[other],
+        ).wait_recv()
         for peer in others_tile:
-            spread(my_tile, other, peer, my_tile).start()
-    for other in others_view:
-        to_view(outgoing, other, everyone.at[my_tile, my_view], out_sem, out_recv, my_view).wait_send()
+            spread(everyone.at[my_tile, other], peer, my_tile).start()
+    ids_down = down(visible_row(visible_ref), BLOCK)
+    for start in range(0, columns, BLOCK):
+        lane_at = lax.broadcasted_iota(jnp.int32, ids_down.shape, 1).astype(jnp.float32) + start
+        hot_back[:, start : start + BLOCK] = jnp.where(ids_down == lane_at, 1.0, 0.0).astype(
+            jnp.bfloat16
+        )
     for peer in others_tile:
-        for view in range(views):
-            copy = spread(peer, view, peer, peer)
-            copy.wait_send()
-            copy.wait_recv()
+        spread(everyone.at[peer], peer, peer).wait_recv()
 
     batch = max(1, min(tiles, 32 // views))
     chunk = batch * views
@@ -405,8 +427,9 @@
                 [held[tile], jnp.zeros((PIX, BLOCK - 2 * SUBS), jnp.float32)], axis=1
             )
         )
+        image_ref[0:3, 0, tile * PIX : (tile + 1) * PIX] = drawn[0:3]
+        image_ref[3:6, 0, tile * PIX : (tile + 1) * PIX] = drawn[SUBS : SUBS + 3]
         drawn = drawn[0:3] + drawn[SUBS : SUBS + 3]
-        image_ref[:, 0, tile * PIX : (tile + 1) * PIX] = drawn
         slope = 2.0 * (drawn - targets_ref[:, 0, tile * PIX : (tile + 1) * PIX])
         high = slope.astype(jnp.bfloat16).astype(jnp.float32)
         stack = jnp.concatenate(
@@ -498,7 +521,7 @@
                 parts[2].append(jnp.where(mine, last_high, 0.0))
                 parts[3].append(jnp.where(mine, last - last_high, 0.0))
             left = jnp.concatenate(parts[0] + parts[1] + parts[2] + parts[3], axis=0)
-            total = total + matmul_nt(left.astype(jnp.bfloat16), hots_wide[tile])
+            total = total + matmul(left.astype(jnp.bfloat16), hots_wide[tile])
         size = pairs * SUBS
         main = (total[0:size] + total[size : 2 * size]).reshape(pairs, SUBS, wide)
         last = total[2 * size : 2 * size + pairs] + total[2 * size + pairs :]
@@ -519,78 +542,61 @@
 
     lax.fori_loop(0, tiles // batch, scatter, 0)
 
-    def to_tile(other, place, slot):
+    def to_tile(source, other, slot, view):
         return pltpu.make_async_remote_copy(
-            src_ref=given.at[other], dst_ref=landed.at[place], send_sem=tile_send.at[other],
-            recv_sem=tile_recv.at[slot], device_id=(my_view, other), device_id_type=MESH,
-        )
-
-    for other in others_tile:
-        to_tile(other, my_tile, my_tile).start()
-    total = given[my_tile]
-    for other in others_tile:
-        to_tile(other, other, other).wait_recv()
-        total = total + landed[other]
-    summed[...] = total
+            src_ref=source, dst_ref=landed.at[view, slot], send_sem=tile_send.at[other],
+            recv_sem=tile_recv.at[view], device_id=(my_view, other), device_id_type=MESH,
+        )
+
+    for view in others_view + [my_view]:
+        for step, other in enumerate(others_tile):
+            to_tile(given.at[other, view], other, tiles - 2 - step, view).start()
+    _, pullback = jax.vjp(lambda source: project(source, cameras), raw)
+    for view in others_view + [my_view]:
+        pltpu.make_async_remote_copy(
+            src_ref=landed.at[view], dst_ref=landed.at[view], send_sem=tile_send.at[0],
+            recv_sem=tile_recv.at[view], device_id=(my_view, others_tile[0]), device_id_type=MESH,
+        ).wait_recv()
+        total = given[my_tile, view]
+        for slot in range(tiles - 1):
+            total = total + landed[view, slot]
+        summed[view] = total
+        if view is not my_view:
+            to_view(
+                summed.at[view], view, arrived_ref.at[my_view], view_send.at[0],
+                view_recv.at[my_view],
+            ).start()
+    arrived_ref[my_view] = summed[my_view]
     for other in others_view:
-        to_view(summed, other, arrived_ref.at[my_view], view_send, view_recv, my_view).start()
-    arrived_ref[my_view] = summed[my_view]
-    for other in others_tile:
-        to_tile(other, my_tile, my_tile).wait_send()
-    for other in others_view:
-        copy = to_view(summed, other, arrived_ref.at[other], view_send, view_recv, other)
-        copy.wait_send()
-        copy.wait_recv()
-
-
-def update_kernel(
-    params_hbm, first_hbm, second_hbm, visible_ref, cameras_ref, picked_ref, arrived_ref, drawn_ref,
-    new_params_hbm, new_first_hbm, new_second_hbm, image_ref,
-    params_ref, first_ref, second_ref, new_params, new_first, new_second, slopes, load_sem, store_sem
-):
-    loads = [
-        pltpu.make_async_copy(params_hbm, params_ref, load_sem.at[0]),
-        pltpu.make_async_copy(first_hbm, first_ref, load_sem.at[1]),
-        pltpu.make_async_copy(second_hbm, second_ref, load_sem.at[2]),
-    ]
-    for load in loads:
-        load.start()
-    image_ref[...] = drawn_ref[...]
-    width, columns = params_ref.shape
-    views, own_rows = visible_ref.shape
+        to_view(
+            summed.at[other], other, arrived_ref.at[other], view_send.at[0], view_recv.at[other]
+        ).wait_recv()
     lower = jnp.concatenate([arrived_ref[view][:, 0:own_rows] for view in range(views)], axis=1)
     upper = jnp.concatenate([arrived_ref[view][:, own_rows:] for view in range(views)], axis=1)
-    cotangent = [lower[row : row + 1] for row in range(8)] + [upper[0:1]]
-    cameras = camera_rows(cameras_ref, own_rows)
-    raw = [picked_ref[row : row + 1, :] for row in range(width)]
-    _, pullback = jax.vjp(lambda source: project(source, cameras), raw)
-    (returned,) = pullback(cotangent)
-    slopes[...] = jnp.ones_like(slopes)
+    (returned,) = pullback([lower[row : row + 1] for row in range(8)] + [upper[0:1]])
+    slopes_ref[...] = jnp.ones_like(slopes_ref)
     for row in range(width):
-        slopes[row : row + 1, :] = returned[row]
-    hot = column_hot(visible_ref, columns)
-    parts = matmul_nt(jnp.concatenate(three_pieces(slopes[...]), axis=0), hot)
-    grad = parts[0:64] + parts[64:128] + parts[128:192]
-    seen = grad[width : width + 1] > 0.5
-    grad = grad[0:width]
-    for load in loads:
-        load.wait()
-    first, second, params = first_ref[...], second_ref[...], params_ref[...]
-    moved_first = beta_first * first + (1.0 - beta_first) * grad
-    moved_second = beta_second * second + (1.0 - beta_second) * grad * grad
-    new_first[...] = jnp.where(seen, moved_first, first)
-    store_first = pltpu.make_async_copy(new_first, new_first_hbm, store_sem.at[1])
-    store_first.start()
-    new_second[...] = jnp.where(seen, moved_second, second)
-    store_second = pltpu.make_async_copy(new_second, new_second_hbm, store_sem.at[2])
-    store_second.start()
-    moved_params = params - learn_rate * moved_first / (jnp.sqrt(moved_second) + adam_eps)
-    new_params[...] = jnp.where(seen, moved_params, params)
-    store_params = pltpu.make_async_copy(new_params, new_params_hbm, store_sem.at[0])
-    store_params.start()
-    store_first.wait()
-    store_second.wait()
-    store_params.wait()
+        slopes_ref[row : row + 1, :] = returned[row]
+    found = matmul(jnp.concatenate(three_pieces(slopes_ref[...]), axis=0), hot_back[...])
+    found = found[0:64] + found[64:128] + found[128:192]
+    grad_ref[...] = found[0:width]
+    seen_ref[...] = found[width : width + 1]
+
+    rest = pl.ds(0, views - 1)
+    to_view(
+        outgoing.at[rest], others_view[0], everyone.at[my_tile, rest], out_sem.at[0],
+        out_recv.at[my_view],
+    ).wait_send()
+    to_view(
+        summed.at[rest], others_view[0], arrived_ref.at[rest], view_send.at[0],
+        view_recv.at[my_view],
+    ).wait_send()
+    for other in others_tile:
+        spread(everyone.at[my_tile], other, my_tile).wait_send()
+        pltpu.make_async_remote_copy(
+            src_ref=given.at[other], dst_ref=given.at[other], send_sem=tile_send.at[other],
+            recv_sem=tile_recv.at[my_view], device_id=(my_view, other), device_id_type=MESH,
+        ).wait_send()
 
 
 def shards(views, tiles, params, first, second, visible, cameras, tile_lists, tile_blocks, targets):
@@ -600,23 +606,24 @@
     packet = (SUBS, 2 * own_rows)
     f32 = jnp.float32
     dma = pltpu.SemaphoreType.DMA
-    image_shape = jax.ShapeDtypeStruct((3, 1, per_device * PIX), f32)
-    picked, arrived, drawn = pl.pallas_call(
+    grad, seen, drawn = pl.pallas_call(
         functools.partial(step_kernel, views, tiles),
         out_shape=[
-            jax.ShapeDtypeStruct((64, views * own_rows), f32),
-            jax.ShapeDtypeStruct((views,) + packet, f32),
-            image_shape,
+            jax.ShapeDtypeStruct(params.shape, f32),
+            jax.ShapeDtypeStruct((1, params.shape[1]), f32),
+            jax.ShapeDtypeStruct((6, 1, per_device * PIX), f32),
         ],
         in_specs=[ANY, VMEM, SMEM, ANY, SMEM, VMEM],
         out_specs=[VMEM, VMEM, VMEM],
         scratch_shapes=[
             pltpu.VMEM(params.shape, f32),
             pltpu.VMEM((per_device, entries), jnp.int32),
+            pltpu.VMEM((64, views * own_rows), f32),
             pltpu.VMEM((views,) + packet, f32),
             pltpu.VMEM((tiles, views) + packet, f32),
+            pltpu.VMEM((views * own_rows, params.shape[1]), jnp.bfloat16),
             pltpu.VMEM((per_device, 4 * own_rows, entries), jnp.bfloat16),
-            pltpu.VMEM((per_device, 2 * own_rows, entries), jnp.bfloat16),
+            pltpu.VMEM((per_device, entries, 2 * own_rows), jnp.bfloat16),
             pltpu.VMEM((per_device, 2 * SUBS, entries), f32),
             pltpu.VMEM((per_device, 2 * SUBS, entries), f32),
             pltpu.VMEM((per_device, blocks, PIX, BLOCK), f32),
@@ -625,29 +632,27 @@
             pltpu.VMEM((per_device, PIX, BLOCK), f32),
             pltpu.VMEM((per_device, PIX, 2 * SUBS), f32),
             pltpu.VMEM((tiles, views) + packet, f32),
-            pltpu.VMEM((tiles, views) + packet, f32),
+            pltpu.VMEM((views, tiles - 1) + packet, f32),
             pltpu.VMEM((views,) + packet, f32),
+            pltpu.VMEM((views,) + packet, f32),
+            pltpu.VMEM((64, views * own_rows), f32),
             dma((2,)),
-            dma((views,)), dma((views,)), dma((tiles, views)), dma((tiles, views)),
-            dma((views,)), dma((views,)), dma((tiles,)), dma((tiles,)),
+            dma((1,)), dma((views,)), dma((tiles,)), dma((tiles,)),
+            dma((1,)), dma((views,)), dma((tiles,)), dma((views,)),
         ],
         compiler_params=pltpu.CompilerParams(
             collective_id=0, has_side_effects=True, vmem_limit_bytes=LIMIT
         ),
         name="render_step",
     )(params, visible, cameras, tile_lists[0], tile_blocks, jnp.transpose(targets, (1, 0, 2)))
-    like = jax.ShapeDtypeStruct(params.shape, f32)
-    new_params, new_first, new_second, rendered = pl.pallas_call(
-        update_kernel,
-        out_shape=[like, like, like, image_shape],
-        in_specs=[ANY, ANY, ANY, VMEM, SMEM, VMEM, VMEM, VMEM],
-        out_specs=[ANY, ANY, ANY, VMEM],
-        scratch_shapes=[pltpu.VMEM(params.shape, f32)] * 6
-        + [pltpu.VMEM((64, views * own_rows), f32), dma((3,)), dma((3,))],
-        compiler_params=pltpu.CompilerParams(vmem_limit_bytes=LIMIT),
-        name="update",
-    )(params, first, second, visible, cameras, picked, arrived, drawn)
-    return (new_params, new_first, new_second, jnp.transpose(rendered, (1, 0, 2)))
+    seen = seen > 0.5
+    moved_first = beta_first * first + (1.0 - beta_first) * grad
+    moved_second = beta_second * second + (1.0 - beta_second) * grad * grad
+    moved_params = params - learn_rate * moved_first / (jnp.sqrt(moved_second) + adam_eps)
+    new_first = jnp.where(seen, moved_first, first)
+    new_second = jnp.where(seen, moved_second, second)
+    new_params = jnp.where(seen, moved_params, params)
+    return (new_params, new_first, new_second, jnp.transpose(drawn[0:3] + drawn[3:6], (1, 0, 2)))
 
 
 def solution(mesh):

time: 43.4 us -> 39.9 us (0.919)
  local copies, waits for them, and re-layouts: 5.31 us -> 0.68 us
  other arithmetic: 0 us -> 3.53 us
  Pallas kernels: 37.1 us -> 34.8 us
    unnamed x16 -> x4, local copies, waits for them, and re-layouts: 5.31 us -> 0.68 us
    pallas_call x1 -> x0, Pallas kernels: 3.21 us -> none  [shards(): pl.pallas_call(update_kernel, out_shape=[like, like, like, image_shape],...]
    select_n x0 -> x1, other arithmetic: none -> 2.2 us  [shards(): new_second = jnp.where(seen, moved_second, second)]
    transpose x0 -> x1, other arithmetic: none -> 1.31 us  [shards(): jnp.transpose(drawn[0:3] + drawn[3:6], (1, 0, 2))]
    pallas_call x1, Pallas kernels: 33.9 us -> 34.8 us  [shards(): pl.pallas_call(functools.partial(step_kernel, views, tiles), out_shape=[j...]
where the time goes in v3:
time: 39.9 us; the launch traced here: 39.6 us
  Pallas kernels  34.8 us (87%)
  other arithmetic  3.53 us (9%)
  local copies, waits for them, and re-layouts  0.68 us (2%)
  between operations  0.66 us (2%)
    pallas_call x1, Pallas kernels, shards(): pl.pallas_call(functools.partial(step_kernel, views, tiles), out_shape=[j...  34.8 us
    select_n x1, other arithmetic, shards(): new_second = jnp.where(seen, moved_second, second)  2.2 us
    transpose x1, other arithmetic, shards(): jnp.transpose(drawn[0:3] + drawn[3:6], (1, 0, 2))  1.31 us

profile of v3, /device:TPU:0, one launch (start us, length us, event | category | flops | bytes accessed | tf_op | source)
XLA Modules:
  0.0 39.6 jit_solution(14660348445075728609)
XLA Ops:
  0.6 0.0 copy-start
  0.6 34.8 %render_step.1 = (f32[59,1024]{1,0:T(8,128)}, f32[1,1024]{1,0:T(1,128)}, f32[6,1,512]{2,1,0:T(1,128)}) custom-call(f32[59,1024]{1,0:T(8,128)} %params_hbm.1, s32[8,64]{1,0:T(8,128)} %visible_ref.1, f32[8,11]{1,0:T(8,128)} %cameras_ref.1, s32[2,1024]{1,0:T(2,128)} %bitcast.4, s32[1,2]{1,0:T(1,128)} %counts_ref.1, f32[3,1,512]{2,1,0:T(1,128)} %bitcast.5), custom_call_target="tpu_custom_call" | custom-call | tf_op jit(solution)/shard_map/render_step/pallas_call | solution.py:609
  35.4 0.0 copy-start.1
  35.4 0.7 %copy-done.1 = f32[1,1024]{1,0:T(1,128)S(1)} copy-done((f32[1,1024]{1,0:T(1,128)S(1)}, f32[1,1024]{1,0:T(1,128)}, u32[]{:S(2)}) %copy-start.1) | copy-done | bytes 4120
  36.1 1.3 %add_bitcast_fusion = f32[1,3,512]{2,0,1:T(1,128)} fusion(f32[6,1,512]{2,1,0:T(1,128)} %get-tuple-element.9), kind=kLoop, calls=%fused_computation.7 | loop fusion | flops 1536 | bytes 18432 | tf_op jit(solution)/shard_map/transpose | solution.py:655
  37.4 0.0 copy-done
  37.5 2.2 %fusion.2 = (f32[59,1024]{1,0:T(8,128)}, f32[59,1024]{1,0:T(8,128)}, f32[59,1024]{1,0:T(8,128)}) fusion(f32[59,1024]{1,0:T(8,128)} %param.10, f32[59,1024]{1,0:T(8,128)} %get-tuple-element.8, pred[1024]{0:T(1024)(128)(4,1)S(1)} %compare_reduce_fusion, f32[59,1024]{1,0:T(8,128)S(1)} %copy-done, f32[59,1024]{1,0:T(8,128)} %param.9), kind=kLoop, calls=%fused_computation.5 | loop fusion | flops 845824 | bytes 1692672 | tf_op jit(solution)/shard_map/jit(_where)/select_n | solution.py:653
  (1 shorter events, 0.0 us)
Async XLA Ops:
  0.6 36.8 %copy-start = (f32[59,1024]{1,0:T(8,128)S(1)}, f32[59,1024]{1,0:T(8,128)}, u32[]{:S(2)}) copy-start(f32[59,1024]{1,0:T(8,128)} %params_hbm.1) | copy-start | bytes 724996
  35.4 0.7 %copy-start.1 = (f32[1,1024]{1,0:T(1,128)S(1)}, f32[1,1024]{1,0:T(1,128)}, u32[]{:S(2)}) copy-start(f32[1,1024]{1,0:T(1,128)} %get-tuple-element.7) | copy-start | bytes 12292

commit v4 on v3

--- a/solution.py
+++ b/solution.py
@@ -233,21 +233,29 @@
     views, tiles, params_hbm, visible_ref, cameras_ref, lists_hbm, counts_ref, targets_ref,
     grad_ref, seen_ref, image_ref,
     params_ref, lists_ref, picked_ref, outgoing, everyone, hot_back, hots, hots_wide, rows, grads,
-    weights, weight_parts, ratios, carried, held, given, landed, summed, arrived_ref, slopes_ref,
-    load_sem, out_sem, out_recv, spread_sem, spread_recv, view_send, view_recv, tile_send, tile_recv
+    weights, weight_parts, ratios, carried, held, given, landed, slopes_ref,
+    load_sem, out_sem, out_recv, back_sem, back_recv
 ):
     my_view, my_tile = lax.axis_index("view"), lax.axis_index("tile")
-    others_view = [lax.rem(my_view + step, views) for step in range(1, views)]
-    others_tile = [lax.rem(my_tile + step, tiles) for step in range(1, tiles)]
-    barrier = pltpu.get_barrier_semaphore()
-    for other in others_view:
-        pl.semaphore_signal(barrier, inc=1, device_id=(other, my_tile), device_id_type=MESH)
-    for other in others_tile:
-        pl.semaphore_signal(barrier, inc=1, device_id=(my_view, other), device_id_type=MESH)
+    owners = views * tiles
+    me = my_tile * views + my_view
+
+    def owner_at(step):
+        other = lax.rem(me + step, owners)
+        return other, lax.rem(other, views), lax.div(other, views)
+
     load_params = pltpu.make_async_copy(params_hbm, params_ref, load_sem.at[0])
     load_lists = pltpu.make_async_copy(lists_hbm, lists_ref, load_sem.at[1])
     load_params.start()
     load_lists.start()
+    barrier = pltpu.get_barrier_semaphore()
+
+    def greet(step, _):
+        _, view, tile = owner_at(step)
+        pl.semaphore_signal(barrier, inc=1, device_id=(view, tile), device_id_type=MESH)
+        return 0
+
+    lax.fori_loop(1, owners, greet, 0)
 
     width, columns = params_ref.shape
     own_rows = visible_ref.shape[1]
@@ -268,27 +276,20 @@
         span = slice(view * own_rows, (view + 1) * own_rows)
         outgoing[view] = jnp.concatenate([lower[:, span], upper[:, span]], axis=1)
 
-    def to_view(source, other, landing, sends, receives):
+    def to_owner(source, landing, sends, receives, view, tile):
         return pltpu.make_async_remote_copy(
-            src_ref=source, dst_ref=landing, send_sem=sends, recv_sem=receives,
-            device_id=(other, my_tile), device_id_type=MESH,
-        )
-
-    def spread(source, other, slot):
-        return pltpu.make_async_remote_copy(
-            src_ref=source, dst_ref=source, send_sem=spread_sem.at[other],
-            recv_sem=spread_recv.at[slot], device_id=(my_view, other), device_id_type=MESH,
-        )
-
-    everyone[my_tile, my_view] = outgoing[my_view]
-    pl.semaphore_wait(barrier, views + tiles - 2)
-    for other in others_view:
-        to_view(
-            outgoing.at[other], other, everyone.at[my_tile, my_view], out_sem.at[0],
-            out_recv.at[my_view],
-        ).start()
-    for other in others_tile:
-        spread(everyone.at[my_tile, my_view], other, my_tile).start()
+            src_ref=source, dst_ref=landing, send_sem=sends.at[0], recv_sem=receives.at[0],
+            device_id=(view, tile), device_id_type=MESH,
+        )
+
+    def send_rows(step, _):
+        _, view, tile = owner_at(step)
+        to_owner(outgoing.at[view], everyone.at[me], out_sem, out_recv, view, tile).start()
+        return 0
+
+    everyone[me] = outgoing[my_view]
+    pl.semaphore_wait(barrier, owners - 1)
+    lax.fori_loop(1, owners, send_rows, 0)
 
     load_lists.wait()
     per_device, entries = lists_ref.shape
@@ -302,28 +303,25 @@
         group = lax.shift_right_logical(ids, wide.bit_length() - 1)
         groups_wide.append(jnp.broadcast_to(group, (SUBS, entries)))
 
-    for other in others_view:
-        to_view(
-            outgoing.at[other], other, everyone.at[my_tile, other], out_sem.at[0],
-            out_recv.at[other],
-        ).wait_recv()
-        for peer in others_tile:
-            spread(everyone.at[my_tile, other], peer, my_tile).start()
     ids_down = down(visible_row(visible_ref), BLOCK)
     for start in range(0, columns, BLOCK):
         lane_at = lax.broadcasted_iota(jnp.int32, ids_down.shape, 1).astype(jnp.float32) + start
         hot_back[:, start : start + BLOCK] = jnp.where(ids_down == lane_at, 1.0, 0.0).astype(
             jnp.bfloat16
         )
-    for peer in others_tile:
-        spread(everyone.at[peer], peer, peer).wait_recv()
+    rest = pl.ds(0, owners - 1)
+    _, next_view, next_tile = owner_at(1)
+    all_rows = to_owner(
+        everyone.at[rest], everyone.at[rest], out_sem, out_recv, next_view, next_tile
+    )
+    all_rows.wait_recv()
 
     batch = max(1, min(tiles, 32 // views))
     chunk = batch * views
     lane = lax.broadcasted_iota(jnp.int32, (chunk * (SUBS + 1), wide), 1)
 
     def gather(index, held_rows):
-        source = everyone[pl.ds(index * batch, batch)].reshape(chunk, SUBS, wide)
+        source = everyone[pl.ds(index * chunk, chunk)]
         last = pltpu.roll(source[:, 0, :], own_rows, 1)
         source = jnp.concatenate([source.reshape(chunk * SUBS, wide), last], axis=0)
         high, middle, low = [piece.astype(jnp.float32) for piece in three_pieces(source)]
@@ -427,9 +425,8 @@
                 [held[tile], jnp.zeros((PIX, BLOCK - 2 * SUBS), jnp.float32)], axis=1
             )
         )
-        image_ref[0:3, 0, tile * PIX : (tile + 1) * PIX] = drawn[0:3]
-        image_ref[3:6, 0, tile * PIX : (tile + 1) * PIX] = drawn[SUBS : SUBS + 3]
         drawn = drawn[0:3] + drawn[SUBS : SUBS + 3]
+        image_ref[:, 0, tile * PIX : (tile + 1) * PIX] = drawn
         slope = 2.0 * (drawn - targets_ref[:, 0, tile * PIX : (tile + 1) * PIX])
         high = slope.astype(jnp.bfloat16).astype(jnp.float32)
         stack = jnp.concatenate(
@@ -535,44 +532,29 @@
             jnp.broadcast_to(last[:, None, :], main.shape),
         )
         for pair in range(pairs):
-            place = index * batch + 2 * pair // views
-            given[place, 2 * pair % views] = even[pair]
-            given[place, 2 * pair % views + 1] = odd[pair]
+            given[index * chunk + 2 * pair] = even[pair]
+            given[index * chunk + 2 * pair + 1] = odd[pair]
         return 0
 
     lax.fori_loop(0, tiles // batch, scatter, 0)
 
-    def to_tile(source, other, slot, view):
-        return pltpu.make_async_remote_copy(
-            src_ref=source, dst_ref=landed.at[view, slot], send_sem=tile_send.at[other],
-            recv_sem=tile_recv.at[view], device_id=(my_view, other), device_id_type=MESH,
-        )
-
-    for view in others_view + [my_view]:
-        for step, other in enumerate(others_tile):
-            to_tile(given.at[other, view], other, tiles - 2 - step, view).start()
+    def send_back(step, _):
+        other, view, tile = owner_at(step)
+        to_owner(given.at[other], landed.at[me], back_sem, back_recv, view, tile).start()
+        return 0
+
+    lax.fori_loop(1, owners, send_back, 0)
+    landed[me] = given[me]
     _, pullback = jax.vjp(lambda source: project(source, cameras), raw)
-    for view in others_view + [my_view]:
-        pltpu.make_async_remote_copy(
-            src_ref=landed.at[view], dst_ref=landed.at[view], send_sem=tile_send.at[0],
-            recv_sem=tile_recv.at[view], device_id=(my_view, others_tile[0]), device_id_type=MESH,
-        ).wait_recv()
-        total = given[my_tile, view]
-        for slot in range(tiles - 1):
-            total = total + landed[view, slot]
-        summed[view] = total
-        if view is not my_view:
-            to_view(
-                summed.at[view], view, arrived_ref.at[my_view], view_send.at[0],
-                view_recv.at[my_view],
-            ).start()
-    arrived_ref[my_view] = summed[my_view]
-    for other in others_view:
-        to_view(
-            summed.at[other], other, arrived_ref.at[other], view_send.at[0], view_recv.at[other]
-        ).wait_recv()
-    lower = jnp.concatenate([arrived_ref[view][:, 0:own_rows] for view in range(views)], axis=1)
-    upper = jnp.concatenate([arrived_ref[view][:, own_rows:] for view in range(views)], axis=1)
+    all_back = to_owner(
+        given.at[rest], landed.at[rest], back_sem, back_recv, next_view, next_tile
+    )
+    all_back.wait_recv()
+    arrived = landed[pl.ds(0, views)]
+    for tile in range(1, tiles):
+        arrived = arrived + landed[pl.ds(tile * views, views)]
+    lower = jnp.concatenate([arrived[view][:, 0:own_rows] for view in range(views)], axis=1)
+    upper = jnp.concatenate([arrived[view][:, own_rows:] for view in range(views)], axis=1)
     (returned,) = pullback([lower[row : row + 1] for row in range(8)] + [upper[0:1]])
     slopes_ref[...] = jnp.ones_like(slopes_ref)
     for row in range(width):
@@ -582,21 +564,24 @@
     grad_ref[...] = found[0:width]
     seen_ref[...] = found[width : width + 1]
 
-    rest = pl.ds(0, views - 1)
-    to_view(
-        outgoing.at[rest], others_view[0], everyone.at[my_tile, rest], out_sem.at[0],
-        out_recv.at[my_view],
-    ).wait_send()
-    to_view(
-        summed.at[rest], others_view[0], arrived_ref.at[rest], view_send.at[0],
-        view_recv.at[my_view],
-    ).wait_send()
-    for other in others_tile:
-        spread(everyone.at[my_tile], other, my_tile).wait_send()
-        pltpu.make_async_remote_copy(
-            src_ref=given.at[other], dst_ref=given.at[other], send_sem=tile_send.at[other],
-            recv_sem=tile_recv.at[my_view], device_id=(my_view, other), device_id_type=MESH,
-        ).wait_send()
+    all_rows.wait_send()
+    all_back.wait_send()
+
+
+def update_kernel(
+    params_ref, first_ref, second_ref, grad_ref, seen_ref, drawn_ref,
+    new_params_ref, new_first_ref, new_second_ref, image_ref
+):
+    grad = grad_ref[...]
+    seen = seen_ref[...] > 0.5
+    first, second, params = first_ref[...], second_ref[...], params_ref[...]
+    moved_first = beta_first * first + (1.0 - beta_first) * grad
+    moved_second = beta_second * second + (1.0 - beta_second) * grad * grad
+    moved_params = params - learn_rate * moved_first / (jnp.sqrt(moved_second) + adam_eps)
+    new_first_ref[...] = jnp.where(seen, moved_first, first)
+    new_second_ref[...] = jnp.where(seen, moved_second, second)
+    new_params_ref[...] = jnp.where(seen, moved_params, params)
+    image_ref[...] = drawn_ref[...]
 
 
 def shards(views, tiles, params, first, second, visible, cameras, tile_lists, tile_blocks, targets):
@@ -606,12 +591,14 @@
     packet = (SUBS, 2 * own_rows)
     f32 = jnp.float32
     dma = pltpu.SemaphoreType.DMA
+    owners = views * tiles
+    image_shape = jax.ShapeDtypeStruct((3, 1, per_device * PIX), f32)
     grad, seen, drawn = pl.pallas_call(
         functools.partial(step_kernel, views, tiles),
         out_shape=[
             jax.ShapeDtypeStruct(params.shape, f32),
             jax.ShapeDtypeStruct((1, params.shape[1]), f32),
-            jax.ShapeDtypeStruct((6, 1, per_device * PIX), f32),
+            image_shape,
         ],
         in_specs=[ANY, VMEM, SMEM, ANY, SMEM, VMEM],
         out_specs=[VMEM, VMEM, VMEM],
@@ -620,7 +607,7 @@
             pltpu.VMEM((per_device, entries), jnp.int32),
             pltpu.VMEM((64, views * own_rows), f32),
             pltpu.VMEM((views,) + packet, f32),
-            pltpu.VMEM((tiles, views) + packet, f32),
+            pltpu.VMEM((owners,) + packet, f32),
             pltpu.VMEM((views * own_rows, params.shape[1]), jnp.bfloat16),
             pltpu.VMEM((per_device, 4 * own_rows, entries), jnp.bfloat16),
             pltpu.VMEM((per_device, entries, 2 * own_rows), jnp.bfloat16),
@@ -631,28 +618,27 @@
             pltpu.VMEM((per_device, blocks, PIX, BLOCK), f32),
             pltpu.VMEM((per_device, PIX, BLOCK), f32),
             pltpu.VMEM((per_device, PIX, 2 * SUBS), f32),
-            pltpu.VMEM((tiles, views) + packet, f32),
-            pltpu.VMEM((views, tiles - 1) + packet, f32),
-            pltpu.VMEM((views,) + packet, f32),
-            pltpu.VMEM((views,) + packet, f32),
+            pltpu.VMEM((owners,) + packet, f32),
+            pltpu.VMEM((owners,) + packet, f32),
             pltpu.VMEM((64, views * own_rows), f32),
             dma((2,)),
-            dma((1,)), dma((views,)), dma((tiles,)), dma((tiles,)),
-            dma((1,)), dma((views,)), dma((tiles,)), dma((views,)),
+            dma((1,)), dma((1,)), dma((1,)), dma((1,)),
         ],
         compiler_params=pltpu.CompilerParams(
             collective_id=0, has_side_effects=True, vmem_limit_bytes=LIMIT
         ),
         name="render_step",
     )(params, visible, cameras, tile_lists[0], tile_blocks, jnp.transpose(targets, (1, 0, 2)))
-    seen = seen > 0.5
-    moved_first = beta_first * first + (1.0 - beta_first) * grad
-    moved_second = beta_second * second + (1.0 - beta_second) * grad * grad
-    moved_params = params - learn_rate * moved_first / (jnp.sqrt(moved_second) + adam_eps)
-    new_first = jnp.where(seen, moved_first, first)
-    new_second = jnp.where(seen, moved_second, second)
-    new_params = jnp.where(seen, moved_params, params)
-    return (new_params, new_first, new_second, jnp.transpose(drawn[0:3] + drawn[3:6], (1, 0, 2)))
+    like = jax.ShapeDtypeStruct(params.shape, f32)
+    new_params, new_first, new_second, rendered = pl.pallas_call(
+        update_kernel,
+        out_shape=[like, like, like, image_shape],
+        in_specs=[VMEM] * 6,
+        out_specs=[VMEM] * 4,
+        compiler_params=pltpu.CompilerParams(vmem_limit_bytes=LIMIT),
+        name="update",
+    )(params, first, second, grad, seen, drawn)
+    return (new_params, new_first, new_second, jnp.transpose(rendered, (1, 0, 2)))
 
 
 def solution(mesh):

time: 39.9 us -> 36 us (0.902)
  other arithmetic: 3.53 us -> 0 us
  local copies, waits for them, and re-layouts: 0.68 us -> 0 us
    select_n x1 -> x0, other arithmetic: 2.2 us -> none  [shards(): new_second = jnp.where(seen, moved_second, second)]
    pallas_call x0 -> x1, Pallas kernels: none -> 2.13 us  [shards(): pl.pallas_call(update_kernel, out_shape=[like, like, like, image_shape],...]
    pallas_call x1, Pallas kernels: 34.8 us -> 33 us  [shards(): pl.pallas_call(functools.partial(step_kernel, views, tiles), out_shape=[j...]
    transpose x1 -> x0, other arithmetic: 1.31 us -> none  [shards(): jnp.transpose(drawn[0:3] + drawn[3:6], (1, 0, 2))]
    unnamed x4 -> x0, local copies, waits for them, and re-layouts: 0.68 us -> none
where the time goes in v4:
time: 36 us; the launch traced here: 35.8 us
  Pallas kernels  35.1 us (98%)
  between operations  0.64 us (2%)
    pallas_call x1, Pallas kernels, shards(): pl.pallas_call(functools.partial(step_kernel, views, tiles), out_shape=[j...  33 us
    pallas_call x1, Pallas kernels, shards(): pl.pallas_call(update_kernel, out_shape=[like, like, like, image_shape],...  2.13 us

profile of v4, /device:TPU:0, one launch (start us, length us, event | category | flops | bytes accessed | tf_op | source)
XLA Modules:
  0.0 35.8 jit_solution(464717386629779356)
XLA Ops:
  0.6 33.0 %render_step.1 = (f32[59,1024]{1,0:T(8,128)}, f32[1,1024]{1,0:T(1,128)}, f32[3,1,512]{2,1,0:T(1,128)}) custom-call(f32[59,1024]{1,0:T(8,128)} %params_ref.1, s32[8,64]{1,0:T(8,128)} %visible_ref.1, f32[8,11]{1,0:T(8,128)} %cameras_ref.1, s32[2,1024]{1,0:T(2,128)} %bitcast.3, s32[1,2]{1,0:T(1,128)} %counts_ref.1, f32[3,1,512]{2,1,0:T(1,128)} %bitcast.4), custom_call_target="tpu_custom_call" | custom-call | tf_op jit(solution)/shard_map/render_step/pallas_call | solution.py:596
  33.6 2.1 %update.1 = (f32[59,1024]{1,0:T(8,128)}, f32[59,1024]{1,0:T(8,128)}, f32[59,1024]{1,0:T(8,128)}, f32[3,1,512]{2,1,0:T(1,128)}) custom-call(f32[59,1024]{1,0:T(8,128)} %params_ref.1, f32[59,1024]{1,0:T(8,128)} %first_ref.1, f32[59,1024]{1,0:T(8,128)} %second_ref.1, f32[59,1024]{1,0:T(8,128)} %get-tuple-element.11.grad_ref, ...), custom_call_target="tpu_custom_call" | custom-call | tf_op jit(solution)/shard_map/update/pallas_call | solution.py:633

commit v5 on v4

--- a/solution.py
+++ b/solution.py
@@ -12,6 +12,7 @@
 BLOCK = 128
 WIN_COLS = 8
 SUBS = 8
+PACK = 5
 MESH = pl.DeviceIdType.MESH
 VMEM = pl.BlockSpec(memory_space=pltpu.VMEM)
 ANY = pl.BlockSpec(memory_space=pl.ANY)
@@ -240,22 +241,21 @@
     owners = views * tiles
     me = my_tile * views + my_view
 
-    def owner_at(step):
-        other = lax.rem(me + step, owners)
-        return other, lax.rem(other, views), lax.div(other, views)
-
+    partners = []
+    for step_view in range(views):
+        view = lax.rem(my_view + step_view, views)
+        for step_tile in range(tiles):
+            if step_view or step_tile:
+                tile = lax.rem(my_tile + step_tile, tiles)
+                partners.append((tile * views + view, view, tile))
     load_params = pltpu.make_async_copy(params_hbm, params_ref, load_sem.at[0])
     load_lists = pltpu.make_async_copy(lists_hbm, lists_ref, load_sem.at[1])
     load_params.start()
     load_lists.start()
     barrier = pltpu.get_barrier_semaphore()
 
-    def greet(step, _):
-        _, view, tile = owner_at(step)
+    for _, view, tile in partners:
         pl.semaphore_signal(barrier, inc=1, device_id=(view, tile), device_id_type=MESH)
-        return 0
-
-    lax.fori_loop(1, owners, greet, 0)
 
     width, columns = params_ref.shape
     own_rows = visible_ref.shape[1]
@@ -270,8 +270,8 @@
     picked_ref[...] = found[0:64] + found[64:128] + found[128:192]
     raw = [picked_ref[row : row + 1, :] for row in range(width)]
     out = project(raw, cameras)
-    lower = jnp.concatenate(out[0:8], axis=0)
-    upper = jnp.concatenate([out[8], jnp.zeros((7, out[8].shape[1]), jnp.float32)], axis=0)
+    lower = jnp.concatenate(out[0:4] + [out[8]], axis=0)
+    upper = jnp.concatenate(out[4:8] + [jnp.zeros_like(out[8])], axis=0)
     for view in range(views):
         span = slice(view * own_rows, (view + 1) * own_rows)
         outgoing[view] = jnp.concatenate([lower[:, span], upper[:, span]], axis=1)
@@ -282,14 +282,10 @@
             device_id=(view, tile), device_id_type=MESH,
         )
 
-    def send_rows(step, _):
-        _, view, tile = owner_at(step)
-        to_owner(outgoing.at[view], everyone.at[me], out_sem, out_recv, view, tile).start()
-        return 0
-
     everyone[me] = outgoing[my_view]
     pl.semaphore_wait(barrier, owners - 1)
-    lax.fori_loop(1, owners, send_rows, 0)
+    for _, view, tile in partners:
+        to_owner(outgoing.at[view], everyone.at[me], out_sem, out_recv, view, tile).start()
 
     load_lists.wait()
     per_device, entries = lists_ref.shape
@@ -310,7 +306,7 @@
             jnp.bfloat16
         )
     rest = pl.ds(0, owners - 1)
-    _, next_view, next_tile = owner_at(1)
+    _, next_view, next_tile = partners[0]
     all_rows = to_owner(
         everyone.at[rest], everyone.at[rest], out_sem, out_recv, next_view, next_tile
     )
@@ -322,7 +318,10 @@
 
     def gather(index, held_rows):
         source = everyone[pl.ds(index * chunk, chunk)]
-        last = pltpu.roll(source[:, 0, :], own_rows, 1)
+        last = source[:, 4, :]
+        source = jnp.concatenate([source, jnp.zeros((chunk, SUBS - PACK, wide), jnp.float32)], axis=1)
+        turned = pltpu.roll(pltpu.roll(source, own_rows, 2), 4, 1)
+        source = jnp.where(lax.broadcasted_iota(jnp.int32, source.shape, 1) < 4, source, turned)
         source = jnp.concatenate([source.reshape(chunk * SUBS, wide), last], axis=0)
         high, middle, low = [piece.astype(jnp.float32) for piece in three_pieces(source)]
         source = jnp.concatenate(
@@ -377,6 +376,7 @@
     ahead = jnp.where((spot < lane_two) | (lane_two >= BLOCK), 1.0, 0.0).astype(jnp.bfloat16)
     behind = jnp.where((spot > lane_two) | (lane_two >= BLOCK), 1.0, 0.0).astype(jnp.bfloat16)
     blocks = entries // BLOCK
+    stride = 2 if blocks % 2 == 0 else 1
 
     carried[...] = jnp.zeros_like(carried)
     held[...] = jnp.zeros_like(held)
@@ -416,7 +416,12 @@
             held[tile] += matmul_nt(parts, jnp.concatenate([both, both], axis=1))
         return 0
 
-    lax.fori_loop(0, blocks, forward, 0)
+    def forward_pair(index, _):
+        for part in range(stride):
+            forward(index * stride + part, 0)
+        return 0
+
+    lax.fori_loop(0, blocks // stride, forward_pair, 0)
 
     slopes, slopes_wide = [], []
     for tile in range(per_device):
@@ -461,12 +466,10 @@
             past = carried[tile]
             inner = pulled - (after[:, 0:BLOCK] + past) * ratios[tile, block]
             carried[tile] = past + after[:, BLOCK:]
-            inner_high, inner_low = two_pieces(inner)
-            sums = matmul(basis, inner_high) + matmul(basis, inner_low)
-            parts = weight_parts[tile, block]
-            tint = matmul(slopes[tile], parts[:, 0:BLOCK])
-            tint_low = matmul(slopes[tile], parts[:, BLOCK:])
-            tint = tint[0:3] + tint[3:6] + tint_low[0:3]
+            sums = matmul(basis, jnp.concatenate(two_pieces(inner), axis=1))
+            sums = sums[:, 0:BLOCK] + sums[:, BLOCK:]
+            tint = matmul(slopes[tile], weight_parts[tile, block])
+            tint = tint[0:3, 0:BLOCK] + tint[3:6, 0:BLOCK] + tint[0:3, BLOCK:]
             mean_x = low[0:1] - middles[tile][0]
             mean_y = low[1:2] - middles[tile][1]
             form_a, form_b, form_c = low[2:3], low[3:4], low[4:5]
@@ -493,7 +496,12 @@
             )
         return 0
 
-    lax.fori_loop(0, blocks, backward, 0)
+    def backward_pair(index, _):
+        for part in range(stride):
+            backward(index * stride + part, 0)
+        return 0
+
+    lax.fori_loop(0, blocks // stride, backward_pair, 0)
 
     pairs = chunk // 2
     lane_pair = lax.broadcasted_iota(jnp.int32, (pairs, SUBS, wide), 2)
@@ -522,28 +530,29 @@
         size = pairs * SUBS
         main = (total[0:size] + total[size : 2 * size]).reshape(pairs, SUBS, wide)
         last = total[2 * size : 2 * size + pairs] + total[2 * size + pairs :]
-        turned = pltpu.roll(last, own_rows, 1)
+        raised = pltpu.roll(main, 4, 1)
+        row_pair = lax.broadcasted_iota(jnp.int32, main.shape, 1)
+        last_turned = pltpu.roll(last, own_rows, 1)
+        low_lane = lane_pair < own_rows
         even = jnp.where(
-            lane_pair < own_rows, main, jnp.broadcast_to(turned[:, None, :], main.shape)
+            row_pair < 4,
+            jnp.where(low_lane, main, pltpu.roll(raised, own_rows, 2)),
+            jnp.broadcast_to(last[:, None, :], main.shape),
         )
         odd = jnp.where(
-            lane_pair < own_rows,
-            pltpu.roll(main, own_rows, 2),
-            jnp.broadcast_to(last[:, None, :], main.shape),
+            row_pair < 4,
+            jnp.where(low_lane, pltpu.roll(main, own_rows, 2), raised),
+            jnp.broadcast_to(last_turned[:, None, :], main.shape),
         )
         for pair in range(pairs):
-            given[index * chunk + 2 * pair] = even[pair]
-            given[index * chunk + 2 * pair + 1] = odd[pair]
+            given[index * chunk + 2 * pair] = even[pair, 0:PACK]
+            given[index * chunk + 2 * pair + 1] = odd[pair, 0:PACK]
         return 0
 
     lax.fori_loop(0, tiles // batch, scatter, 0)
 
-    def send_back(step, _):
-        other, view, tile = owner_at(step)
+    for other, view, tile in partners:
         to_owner(given.at[other], landed.at[me], back_sem, back_recv, view, tile).start()
-        return 0
-
-    lax.fori_loop(1, owners, send_back, 0)
     landed[me] = given[me]
     _, pullback = jax.vjp(lambda source: project(source, cameras), raw)
     all_back = to_owner(
@@ -555,7 +564,11 @@
         arrived = arrived + landed[pl.ds(tile * views, views)]
     lower = jnp.concatenate([arrived[view][:, 0:own_rows] for view in range(views)], axis=1)
     upper = jnp.concatenate([arrived[view][:, own_rows:] for view in range(views)], axis=1)
-    (returned,) = pullback([lower[row : row + 1] for row in range(8)] + [upper[0:1]])
+    (returned,) = pullback(
+        [lower[row : row + 1] for row in range(4)]
+        + [upper[row : row + 1] for row in range(4)]
+        + [lower[4:5]]
+    )
     slopes_ref[...] = jnp.ones_like(slopes_ref)
     for row in range(width):
         slopes_ref[row : row + 1, :] = returned[row]
@@ -588,7 +601,7 @@
     own_rows = visible.shape[1]
     per_device, entries = tile_lists.shape[1:]
     blocks = entries // BLOCK
-    packet = (SUBS, 2 * own_rows)
+    packet = (PACK, 2 * own_rows)
     f32 = jnp.float32
     dma = pltpu.SemaphoreType.DMA
     owners = views * tiles

time: 36 us -> 32.9 us (0.914)
  Pallas kernels: 35.1 us -> 32 us
    pallas_call x1, Pallas kernels: 33 us -> 29.9 us  [shards(): pl.pallas_call(functools.partial(step_kernel, views, tiles), out_shape=[j...]
where the time goes in v5:
time: 32.9 us; the launch traced here: 32.6 us
  Pallas kernels  32 us (97%)
  between operations  0.64 us (2%)
    pallas_call x1, Pallas kernels, shards(): pl.pallas_call(functools.partial(step_kernel, views, tiles), out_shape=[j...  29.9 us
    pallas_call x1, Pallas kernels, shards(): pl.pallas_call(update_kernel, out_shape=[like, like, like, image_shape],...  2.13 us

profile of v5, /device:TPU:0, one launch (start us, length us, event | category | flops | bytes accessed | tf_op | source)
XLA Modules:
  0.0 32.6 jit_solution(12040975085149566080)
XLA Ops:
  0.6 29.9 %render_step.1 = (f32[59,1024]{1,0:T(8,128)}, f32[1,1024]{1,0:T(1,128)}, f32[3,1,512]{2,1,0:T(1,128)}) custom-call(f32[59,1024]{1,0:T(8,128)} %params_ref.1, s32[8,64]{1,0:T(8,128)} %visible_ref.1, f32[8,11]{1,0:T(8,128)} %cameras_ref.1, s32[2,1024]{1,0:T(2,128)} %bitcast.3, s32[1,2]{1,0:T(1,128)} %counts_ref.1, f32[3,1,512]{2,1,0:T(1,128)} %bitcast.4), custom_call_target="tpu_custom_call" | custom-call | tf_op jit(solution)/shard_map/render_step/pallas_call | solution.py:609
  30.5 2.1 %update.1 = (f32[59,1024]{1,0:T(8,128)}, f32[59,1024]{1,0:T(8,128)}, f32[59,1024]{1,0:T(8,128)}, f32[3,1,512]{2,1,0:T(1,128)}) custom-call(f32[59,1024]{1,0:T(8,128)} %params_ref.1, f32[59,1024]{1,0:T(8,128)} %first_ref.1, f32[59,1024]{1,0:T(8,128)} %second_ref.1, f32[59,1024]{1,0:T(8,128)} %get-tuple-element.11.grad_ref, ...), custom_call_target="tpu_custom_call" | custom-call | tf_op jit(solution)/shard_map/update/pallas_call | solution.py:646

commit v6 on v5

--- a/solution.py
+++ b/solution.py
@@ -231,9 +231,9 @@
 
 
 def step_kernel(
-    views, tiles, params_hbm, visible_ref, cameras_ref, lists_hbm, counts_ref, targets_ref,
+    views, tiles, params_hbm, visible_hbm, cameras_hbm, lists_hbm, counts_hbm, targets_hbm,
     grad_ref, seen_ref, image_ref,
-    params_ref, lists_ref, picked_ref, outgoing, everyone, hot_back, hots, hots_wide, rows, grads,
+    params_ref, visible_ref, cameras_ref, lists_ref, counts_ref, targets_ref, picked_ref, outgoing, everyone, hot_back, hots, hots_wide, rows, grads,
     weights, weight_parts, ratios, carried, held, given, landed, slopes_ref,
     load_sem, out_sem, out_recv, back_sem, back_recv
 ):
@@ -248,10 +248,16 @@
             if step_view or step_tile:
                 tile = lax.rem(my_tile + step_tile, tiles)
                 partners.append((tile * views + view, view, tile))
-    load_params = pltpu.make_async_copy(params_hbm, params_ref, load_sem.at[0])
-    load_lists = pltpu.make_async_copy(lists_hbm, lists_ref, load_sem.at[1])
-    load_params.start()
-    load_lists.start()
+    pairs = (
+        (visible_hbm, visible_ref), (cameras_hbm, cameras_ref), (params_hbm, params_ref),
+        (lists_hbm, lists_ref), (counts_hbm, counts_ref), (targets_hbm, targets_ref),
+    )
+    loads = [
+        pltpu.make_async_copy(source, held_at, load_sem.at[place])
+        for place, (source, held_at) in enumerate(pairs)
+    ]
+    for load in loads:
+        load.start()
     barrier = pltpu.get_barrier_semaphore()
 
     for _, view, tile in partners:
@@ -260,9 +266,11 @@
     width, columns = params_ref.shape
     own_rows = visible_ref.shape[1]
     wide = 2 * own_rows
+    loads[0].wait()
     hot = column_hot(visible_ref, columns)
+    loads[1].wait()
     cameras = camera_rows(cameras_ref, own_rows)
-    load_params.wait()
+    loads[2].wait()
     padded = jnp.concatenate(
         [params_ref[...], jnp.zeros((64 - width, columns), jnp.float32)], axis=0
     )
@@ -287,7 +295,8 @@
     for _, view, tile in partners:
         to_owner(outgoing.at[view], everyone.at[me], out_sem, out_recv, view, tile).start()
 
-    load_lists.wait()
+    for load in loads[3:]:
+        load.wait()
     per_device, entries = lists_ref.shape
     groups, groups_wide = [], []
     for tile in range(per_device):
@@ -374,9 +383,10 @@
     )
     lane_two = lax.broadcasted_iota(jnp.int32, (2 * BLOCK, 2 * BLOCK), 1)
     ahead = jnp.where((spot < lane_two) | (lane_two >= BLOCK), 1.0, 0.0).astype(jnp.bfloat16)
-    behind = jnp.where((spot > lane_two) | (lane_two >= BLOCK), 1.0, 0.0).astype(jnp.bfloat16)
+    behind = jnp.where((spot > lane_two) | (lane_two >= BLOCK), 1.0, 0.0)[0:BLOCK]
+    behind = behind.astype(jnp.bfloat16)
     blocks = entries // BLOCK
-    stride = 2 if blocks % 2 == 0 else 1
+    stride = 4 if blocks % 4 == 0 else 1
 
     carried[...] = jnp.zeros_like(carried)
     held[...] = jnp.zeros_like(held)
@@ -409,7 +419,7 @@
             ratios[tile, block] = alpha * jnp.exp(-decay)
             weights[tile, block] = weight
             parts = jnp.concatenate(two_pieces(weight), axis=1)
-            weight_parts[tile, block] = parts
+            weight_parts[tile, block] = parts[:, 0:BLOCK]
             colour = jnp.concatenate([low[6:8], up[0:1], jnp.zeros((5, BLOCK), jnp.float32)], axis=0)
             high = colour.astype(jnp.bfloat16).astype(jnp.float32)
             both = jnp.concatenate([high, colour - high], axis=0).astype(jnp.bfloat16)
@@ -462,14 +472,13 @@
                 [high, high, colour - high, jnp.zeros((7, BLOCK), jnp.float32)], axis=0
             ).astype(jnp.bfloat16)
             pulled = matmul(slopes_wide[tile], both) * weights[tile, block]
-            after = matmul(jnp.concatenate(two_pieces(pulled), axis=1), behind)
+            after = matmul(pulled.astype(jnp.bfloat16), behind)
             past = carried[tile]
             inner = pulled - (after[:, 0:BLOCK] + past) * ratios[tile, block]
             carried[tile] = past + after[:, BLOCK:]
-            sums = matmul(basis, jnp.concatenate(two_pieces(inner), axis=1))
-            sums = sums[:, 0:BLOCK] + sums[:, BLOCK:]
+            sums = matmul(basis, inner.astype(jnp.bfloat16))
             tint = matmul(slopes[tile], weight_parts[tile, block])
-            tint = tint[0:3, 0:BLOCK] + tint[3:6, 0:BLOCK] + tint[0:3, BLOCK:]
+            tint = tint[0:3] + tint[3:6]
             mean_x = low[0:1] - middles[tile][0]
             mean_y = low[1:2] - middles[tile][1]
             form_a, form_b, form_c = low[2:3], low[3:4], low[4:5]
@@ -613,11 +622,15 @@
             jax.ShapeDtypeStruct((1, params.shape[1]), f32),
             image_shape,
         ],
-        in_specs=[ANY, VMEM, SMEM, ANY, SMEM, VMEM],
+        in_specs=[ANY] * 6,
         out_specs=[VMEM, VMEM, VMEM],
         scratch_shapes=[
             pltpu.VMEM(params.shape, f32),
+            pltpu.VMEM(visible.shape, jnp.int32),
+            pltpu.SMEM(cameras.shape, f32),
             pltpu.VMEM((per_device, entries), jnp.int32),
+            pltpu.SMEM(tile_blocks.shape, jnp.int32),
+            pltpu.VMEM((3, 1, per_device * PIX), f32),
             pltpu.VMEM((64, views * own_rows), f32),
             pltpu.VMEM((views,) + packet, f32),
             pltpu.VMEM((owners,) + packet, f32),
@@ -627,14 +640,14 @@
             pltpu.VMEM((per_device, 2 * SUBS, entries), f32),
             pltpu.VMEM((per_device, 2 * SUBS, entries), f32),
             pltpu.VMEM((per_device, blocks, PIX, BLOCK), f32),
-            pltpu.VMEM((per_device, blocks, PIX, 2 * BLOCK), jnp.bfloat16),
+            pltpu.VMEM((per_device, blocks, PIX, BLOCK), jnp.bfloat16),
             pltpu.VMEM((per_device, blocks, PIX, BLOCK), f32),
             pltpu.VMEM((per_device, PIX, BLOCK), f32),
             pltpu.VMEM((per_device, PIX, 2 * SUBS), f32),
             pltpu.VMEM((owners,) + packet, f32),
             pltpu.VMEM((owners,) + packet, f32),
             pltpu.VMEM((64, views * own_rows), f32),
-            dma((2,)),
+            dma((6,)),
             dma((1,)), dma((1,)), dma((1,)), dma((1,)),
         ],
         compiler_params=pltpu.CompilerParams(

time: 32.9 us -> 30.8 us (0.936)
  Pallas kernels: 32 us -> 30 us
    pallas_call x1, Pallas kernels: 29.9 us -> 27.9 us  [shards(): pl.pallas_call(functools.partial(step_kernel, views, tiles), out_shape=[j...]
where the time goes in v6:
time: 30.8 us; the launch traced here: 30.6 us
  Pallas kernels  30 us (97%)
  between operations  0.64 us (2%)
    pallas_call x1, Pallas kernels, shards(): pl.pallas_call(functools.partial(step_kernel, views, tiles), out_shape=[j...  27.9 us
    pallas_call x1, Pallas kernels, shards(): pl.pallas_call(update_kernel, out_shape=[like, like, like, image_shape],...  2.13 us

profile of v6, /device:TPU:0, one launch (start us, length us, event | category | flops | bytes accessed | tf_op | source)
XLA Modules:
  0.0 30.6 jit_solution(15765000882260785032)
XLA Ops:
  0.6 27.9 %render_step.1 = (f32[59,1024]{1,0:T(8,128)}, f32[1,1024]{1,0:T(1,128)}, f32[3,1,512]{2,1,0:T(1,128)}) custom-call(f32[59,1024]{1,0:T(8,128)} %params_ref.1, s32[8,64]{1,0:T(8,128)} %visible_hbm.1, f32[8,11]{1,0:T(8,128)} %cameras_hbm.1, s32[2,1024]{1,0:T(2,128)} %bitcast.3, s32[1,2]{1,0:T(1,128)} %counts_hbm.1, f32[3,1,512]{2,1,0:T(1,128)} %bitcast.4), custom_call_target="tpu_custom_call" | custom-call | tf_op jit(solution)/shard_map/render_step/pallas_call | solution.py:618
  28.5 2.1 %update.1 = (f32[59,1024]{1,0:T(8,128)}, f32[59,1024]{1,0:T(8,128)}, f32[59,1024]{1,0:T(8,128)}, f32[3,1,512]{2,1,0:T(1,128)}) custom-call(f32[59,1024]{1,0:T(8,128)} %params_ref.1, f32[59,1024]{1,0:T(8,128)} %first_ref.1, f32[59,1024]{1,0:T(8,128)} %second_ref.1, f32[59,1024]{1,0:T(8,128)} %get-tuple-element.11.grad_ref, ...), custom_call_target="tpu_custom_call" | custom-call | tf_op jit(solution)/shard_map/update/pallas_call | solution.py:659

commit v7 on v6

--- a/solution.py
+++ b/solution.py
@@ -203,12 +203,15 @@
 
 def camera_rows(cameras_ref, own_rows):
     views = cameras_ref.shape[0]
-    lane = lax.broadcasted_iota(jnp.int32, (1, views * own_rows), 1)
+    shape = (views // 2, 2 * own_rows)
+    number = 2 * lax.broadcasted_iota(jnp.int32, shape, 0) + jnp.where(
+        lax.broadcasted_iota(jnp.int32, shape, 1) >= own_rows, 1, 0
+    )
     rows = []
     for entry in range(11):
-        row = jnp.full(lane.shape, cameras_ref[0, entry], jnp.float32)
+        row = jnp.full(shape, cameras_ref[0, entry], jnp.float32)
         for view in range(1, views):
-            row = jnp.where(lane >= view * own_rows, cameras_ref[view, entry], row)
+            row = jnp.where(number >= view, cameras_ref[view, entry], row)
         rows.append(row)
     return rows
 
@@ -234,7 +237,7 @@
     views, tiles, params_hbm, visible_hbm, cameras_hbm, lists_hbm, counts_hbm, targets_hbm,
     grad_ref, seen_ref, image_ref,
     params_ref, visible_ref, cameras_ref, lists_ref, counts_ref, targets_ref, picked_ref, outgoing, everyone, hot_back, hots, hots_wide, rows, grads,
-    weights, weight_parts, ratios, carried, held, given, landed, slopes_ref,
+    weights, weight_parts, ratios, carried, held, given, landed, slopes_ref, folded,
     load_sem, out_sem, out_recv, back_sem, back_recv
 ):
     my_view, my_tile = lax.axis_index("view"), lax.axis_index("tile")
@@ -275,14 +278,23 @@
         [params_ref[...], jnp.zeros((64 - width, columns), jnp.float32)], axis=0
     )
     found = matmul(jnp.concatenate(three_pieces(padded), axis=0), hot)
-    picked_ref[...] = found[0:64] + found[64:128] + found[128:192]
-    raw = [picked_ref[row : row + 1, :] for row in range(width)]
+    found = found[0:64] + found[64:128] + found[128:192]
+    folds = views // 2
+    for fold in range(folds):
+        picked_ref[fold * 64 : (fold + 1) * 64, :] = found[:, fold * wide : (fold + 1) * wide]
+    raw = [picked_ref[pl.ds(row, folds, stride=64), :] for row in range(width)]
     out = project(raw, cameras)
-    lower = jnp.concatenate(out[0:4] + [out[8]], axis=0)
-    upper = jnp.concatenate(out[4:8] + [jnp.zeros_like(out[8])], axis=0)
-    for view in range(views):
-        span = slice(view * own_rows, (view + 1) * own_rows)
-        outgoing[view] = jnp.concatenate([lower[:, span], upper[:, span]], axis=1)
+    for row in range(9):
+        folded[pl.ds(row, folds, stride=2 * SUBS), :] = out[row]
+    low_lane = lax.broadcasted_iota(jnp.int32, (4, wide), 1) < own_rows
+    for fold in range(folds):
+        first = folded[fold * 2 * SUBS : fold * 2 * SUBS + 4, :]
+        second = folded[fold * 2 * SUBS + 4 : fold * 2 * SUBS + 8, :]
+        last = folded[fold * 2 * SUBS + 8 : fold * 2 * SUBS + 9, :]
+        outgoing[2 * fold, 0:4] = jnp.where(low_lane, first, pltpu.roll(second, own_rows, 1))
+        outgoing[2 * fold, 4:5] = last
+        outgoing[2 * fold + 1, 0:4] = jnp.where(low_lane, pltpu.roll(first, own_rows, 1), second)
+        outgoing[2 * fold + 1, 4:5] = pltpu.roll(last, own_rows, 1)
 
     def to_owner(source, landing, sends, receives, view, tile):
         return pltpu.make_async_remote_copy(
@@ -542,15 +554,15 @@
         raised = pltpu.roll(main, 4, 1)
         row_pair = lax.broadcasted_iota(jnp.int32, main.shape, 1)
         last_turned = pltpu.roll(last, own_rows, 1)
-        low_lane = lane_pair < own_rows
+        low_pair = lane_pair < own_rows
         even = jnp.where(
             row_pair < 4,
-            jnp.where(low_lane, main, pltpu.roll(raised, own_rows, 2)),
+            jnp.where(low_pair, main, pltpu.roll(raised, own_rows, 2)),
             jnp.broadcast_to(last[:, None, :], main.shape),
         )
         odd = jnp.where(
             row_pair < 4,
-            jnp.where(low_lane, pltpu.roll(main, own_rows, 2), raised),
+            jnp.where(low_pair, pltpu.roll(main, own_rows, 2), raised),
             jnp.broadcast_to(last_turned[:, None, :], main.shape),
         )
         for pair in range(pairs):
@@ -571,18 +583,23 @@
     arrived = landed[pl.ds(0, views)]
     for tile in range(1, tiles):
         arrived = arrived + landed[pl.ds(tile * views, views)]
-    lower = jnp.concatenate([arrived[view][:, 0:own_rows] for view in range(views)], axis=1)
-    upper = jnp.concatenate([arrived[view][:, own_rows:] for view in range(views)], axis=1)
-    (returned,) = pullback(
-        [lower[row : row + 1] for row in range(4)]
-        + [upper[row : row + 1] for row in range(4)]
-        + [lower[4:5]]
-    )
+    for fold in range(folds):
+        even, odd = arrived[2 * fold], arrived[2 * fold + 1]
+        odd_turned = pltpu.roll(odd, own_rows, 1)
+        even_turned = pltpu.roll(even, own_rows, 1)
+        begin = fold * 2 * SUBS
+        folded[begin : begin + 4, :] = jnp.where(low_lane, even[0:4], odd_turned[0:4])
+        folded[begin + 4 : begin + 8, :] = jnp.where(low_lane, even_turned[0:4], odd[0:4])
+        folded[begin + 8 : begin + 9, :] = jnp.where(low_lane[0:1], even[4:5], odd_turned[4:5])
+    (returned,) = pullback([folded[pl.ds(row, folds, stride=2 * SUBS), :] for row in range(9)])
     slopes_ref[...] = jnp.ones_like(slopes_ref)
     for row in range(width):
-        slopes_ref[row : row + 1, :] = returned[row]
-    found = matmul(jnp.concatenate(three_pieces(slopes_ref[...]), axis=0), hot_back[...])
-    found = found[0:64] + found[64:128] + found[128:192]
+        slopes_ref[pl.ds(row, folds, stride=64), :] = returned[row]
+    slopes = jnp.concatenate(
+        [slopes_ref[fold * 64 : (fold + 1) * 64, :] for fold in range(folds)], axis=1
+    )
+    found = matmul(jnp.concatenate(two_pieces(slopes), axis=0), hot_back[...])
+    found = found[0:64] + found[64:128]
     grad_ref[...] = found[0:width]
     seen_ref[...] = found[width : width + 1]
 
@@ -631,7 +648,7 @@
             pltpu.VMEM((per_device, entries), jnp.int32),
             pltpu.SMEM(tile_blocks.shape, jnp.int32),
             pltpu.VMEM((3, 1, per_device * PIX), f32),
-            pltpu.VMEM((64, views * own_rows), f32),
+            pltpu.VMEM((64 * views // 2, 2 * own_rows), f32),
             pltpu.VMEM((views,) + packet, f32),
             pltpu.VMEM((owners,) + packet, f32),
             pltpu.VMEM((views * own_rows, params.shape[1]), jnp.bfloat16),
@@ -646,7 +663,8 @@
             pltpu.VMEM((per_device, PIX, 2 * SUBS), f32),
             pltpu.VMEM((owners,) + packet, f32),
             pltpu.VMEM((owners,) + packet, f32),
-            pltpu.VMEM((64, views * own_rows), f32),
+            pltpu.VMEM((64 * views // 2, 2 * own_rows), f32),
+            pltpu.VMEM((SUBS * views, 2 * own_rows), f32),
             dma((6,)),
             dma((1,)), dma((1,)), dma((1,)), dma((1,)),
         ],

time: 30.8 us -> 30.5 us (level)
    pallas_call x1, Pallas kernels: 27.9 us -> 27.5 us  [shards(): pl.pallas_call(functools.partial(step_kernel, views, tiles), out_shape=[j...]
where the time goes in v7:
time: 30.5 us; the launch traced here: 30.3 us
  Pallas kernels  29.7 us (97%)
  between operations  0.64 us (2%)
    pallas_call x1, Pallas kernels, shards(): pl.pallas_call(functools.partial(step_kernel, views, tiles), out_shape=[j...  27.5 us
    pallas_call x1, Pallas kernels, shards(): pl.pallas_call(update_kernel, out_shape=[like, like, like, image_shape],...  2.13 us

profile of v7, /device:TPU:0, one launch (start us, length us, event | category | flops | bytes accessed | tf_op | source)
XLA Modules:
  0.0 30.3 jit_solution(12579737596555183076)
XLA Ops:
  0.6 27.5 %render_step.1 = (f32[59,1024]{1,0:T(8,128)}, f32[1,1024]{1,0:T(1,128)}, f32[3,1,512]{2,1,0:T(1,128)}) custom-call(f32[59,1024]{1,0:T(8,128)} %params_ref.1, s32[8,64]{1,0:T(8,128)} %visible_hbm.1, f32[8,11]{1,0:T(8,128)} %cameras_hbm.1, s32[2,1024]{1,0:T(2,128)} %bitcast.3, s32[1,2]{1,0:T(1,128)} %counts_hbm.1, f32[3,1,512]{2,1,0:T(1,128)} %bitcast.4), custom_call_target="tpu_custom_call" | custom-call | tf_op jit(solution)/shard_map/render_step/pallas_call | solution.py:635
  28.2 2.1 %update.1 = (f32[59,1024]{1,0:T(8,128)}, f32[59,1024]{1,0:T(8,128)}, f32[59,1024]{1,0:T(8,128)}, f32[3,1,512]{2,1,0:T(1,128)}) custom-call(f32[59,1024]{1,0:T(8,128)} %params_ref.1, f32[59,1024]{1,0:T(8,128)} %first_ref.1, f32[59,1024]{1,0:T(8,128)} %second_ref.1, f32[59,1024]{1,0:T(8,128)} %get-tuple-element.11.grad_ref, ...), custom_call_target="tpu_custom_call" | custom-call | tf_op jit(solution)/shard_map/update/pallas_call | solution.py:677

commit v8 on v7

--- a/solution.py
+++ b/solution.py
@@ -398,7 +398,7 @@
     behind = jnp.where((spot > lane_two) | (lane_two >= BLOCK), 1.0, 0.0)[0:BLOCK]
     behind = behind.astype(jnp.bfloat16)
     blocks = entries // BLOCK
-    stride = 4 if blocks % 4 == 0 else 1
+    stride = 8 if blocks % 8 == 0 else 1
 
     carried[...] = jnp.zeros_like(carried)
     held[...] = jnp.zeros_like(held)

time: 30.5 us -> 29.8 us (0.977)
  Pallas kernels: 29.7 us -> 29 us
    pallas_call x1, Pallas kernels: 27.5 us -> 26.8 us  [shards(): pl.pallas_call(functools.partial(step_kernel, views, tiles), out_shape=[j...]
where the time goes in v8:
time: 29.8 us; the launch traced here: 29.6 us
  Pallas kernels  29 us (97%)
  between operations  0.64 us (2%)
    pallas_call x1, Pallas kernels, shards(): pl.pallas_call(functools.partial(step_kernel, views, tiles), out_shape=[j...  26.8 us
    pallas_call x1, Pallas kernels, shards(): pl.pallas_call(update_kernel, out_shape=[like, like, like, image_shape],...  2.13 us

profile of v8, /device:TPU:0, one launch (start us, length us, event | category | flops | bytes accessed | tf_op | source)
XLA Modules:
  0.0 29.6 jit_solution(15061693322495458484)
XLA Ops:
  0.6 26.8 %render_step.1 = (f32[59,1024]{1,0:T(8,128)}, f32[1,1024]{1,0:T(1,128)}, f32[3,1,512]{2,1,0:T(1,128)}) custom-call(f32[59,1024]{1,0:T(8,128)} %params_ref.1, s32[8,64]{1,0:T(8,128)} %visible_hbm.1, f32[8,11]{1,0:T(8,128)} %cameras_hbm.1, s32[2,1024]{1,0:T(2,128)} %bitcast.3, s32[1,2]{1,0:T(1,128)} %counts_hbm.1, f32[3,1,512]{2,1,0:T(1,128)} %bitcast.4), custom_call_target="tpu_custom_call" | custom-call | tf_op jit(solution)/shard_map/render_step/pallas_call | solution.py:635
  27.5 2.1 %update.1 = (f32[59,1024]{1,0:T(8,128)}, f32[59,1024]{1,0:T(8,128)}, f32[59,1024]{1,0:T(8,128)}, f32[3,1,512]{2,1,0:T(1,128)}) custom-call(f32[59,1024]{1,0:T(8,128)} %params_ref.1, f32[59,1024]{1,0:T(8,128)} %first_ref.1, f32[59,1024]{1,0:T(8,128)} %second_ref.1, f32[59,1024]{1,0:T(8,128)} %get-tuple-element.11.grad_ref, ...), custom_call_target="tpu_custom_call" | custom-call | tf_op jit(solution)/shard_map/update/pallas_call | solution.py:677
